TPU v7x, 256 devices: a whole 4x4x8 slice. The times are simulated.
256 devices in a mesh: tile: 64 (over y_lo, x, z), chan: 4 (over y_hi, core).
Axes of the slice: x: 4, y: 4 (y_hi: 2, y_lo: 2; y = y_hi * 2 + y_lo), z: 8, core: 2. Of those that a mesh axis runs over, the one named last changes fastest.
Arguments:
- inputs: bfloat16 [192, 256, 64], P('tile', 'chan'), may hold values from -6 to 6
- prior_hidden_state: bfloat16 [192, 256, 64], P('tile', 'chan'), may hold values from -1 to 1
- cell_prev: float32 [192, 256, 64], P('tile', 'chan'), may hold values from -6 to 6
- kernel: bfloat16 [9, 4, 256, 512], P(None, None, 'chan'), may hold values from -0.09375 to 0.09375
- gate_bias: float32 [4, 256], P(None, 'chan'), may hold values from -3 to 3
- hidden_upstream: bfloat16 [192, 256, 64], P('tile', 'chan'), may hold values from -6 to 6
- cell_upstream: float32 [192, 256, 64], P('tile', 'chan'), may hold values from -6 to 6
- edge_source: int32 [192, 4], replicated, may hold values from 0 to 191
- edge_code: int32 [192, 4], replicated, may hold values from 0 to 7
- corner_source: int32 [192, 4], replicated, may hold values from 0 to 191
- corner_code: int32 [192, 4], replicated, may hold values from 0 to 3
Outputs:
- hidden_new: bfloat16 [192, 256, 64], P('tile', 'chan')
- cell_new: float32 [192, 256, 64], P('tile', 'chan')
- kernel_grad: float32 [9, 4, 256, 512], P(None, None, 'chan')
- bias_grad: float32 [4, 256], P(None, 'chan')
- input_grad: bfloat16 [192, 256, 64], P('tile', 'chan')
- hidden_grad: bfloat16 [192, 256, 64], P('tile', 'chan')
- cell_grad: float32 [192, 256, 64], P('tile', 'chan')
All inputs are finite; a program needn't handle non-finite values.
Results may differ from a plain program's by a relative error of at most 0.0055.
Values may be sent and summed in bfloat16 or wider, within the bound.
A program may use at most 192 MiB of HBM per device.

v0:
```python
import jax
import jax.numpy as jnp
from jax import lax
from jax.sharding import PartitionSpec as P

TS = 8


def rim_parts(tile_field):
    sides = jnp.stack(
        [
            tile_field[:, :, 0, :],
            tile_field[:, :, :, -1],
            tile_field[:, :, -1, :],
            tile_field[:, :, :, 0],
        ],
        axis=1,
    )
    corners = jnp.stack(
        [
            tile_field[:, :, 0, 0],
            tile_field[:, :, 0, -1],
            tile_field[:, :, -1, -1],
            tile_field[:, :, -1, 0],
        ],
        axis=1,
    )
    return (sides, corners)


def cycle_parts(padded):
    sides = jnp.stack(
        [
            padded[:, :, 0, 1:-1],
            padded[:, :, 1:-1, -1],
            padded[:, :, -1, 1:-1],
            padded[:, :, 1:-1, 0],
        ],
        axis=1,
    )
    corners = jnp.stack(
        [padded[:, :, 0, 0], padded[:, :, 0, -1], padded[:, :, -1, -1], padded[:, :, -1, 0]], axis=1
    )
    return (sides, corners)


def mirror_edge_order(edges, codes):
    flags = (codes % 2 == 1)[:, :, None, None]
    return jnp.where(flags, edges[..., ::-1], edges)


def assemble(tile_field, edges, corners):
    top_row = jnp.concatenate([corners[:, 0, :, None], edges[:, 0], corners[:, 1, :, None]], axis=2)
    bottom_row = jnp.concatenate(
        [corners[:, 3, :, None], edges[:, 2], corners[:, 2, :, None]], axis=2
    )
    middle = jnp.concatenate(
        [edges[:, 3][:, :, :, None], tile_field, edges[:, 1][:, :, :, None]], axis=3
    )
    return jnp.concatenate([top_row[:, :, None, :], middle, bottom_row[:, :, None, :]], axis=2)


def place_rims(interior, side_sum, corner_sum):
    result = interior
    result = result.at[:, :, 0, :].add(side_sum[:, 0])
    result = result.at[:, :, :, -1].add(side_sum[:, 1])
    result = result.at[:, :, -1, :].add(side_sum[:, 2])
    result = result.at[:, :, :, 0].add(side_sum[:, 3])
    result = result.at[:, :, 0, 0].add(corner_sum[:, 0])
    result = result.at[:, :, 0, -1].add(corner_sum[:, 1])
    result = result.at[:, :, -1, -1].add(corner_sum[:, 2])
    result = result.at[:, :, -1, 0].add(corner_sum[:, 3])
    return result


def halo_picker(own_esrc, own_ecode, own_csrc, own_ccode):

    def picker(carry, pieces, start):
        sides, corners = pieces
        nrows = sides.shape[0]
        slots_range = jnp.arange(nrows * 4, dtype=jnp.int32)
        edge_key = own_esrc * 4 + own_ecode // 2
        edge_chooser = (edge_key[:, :, None] == slots_range[None, None, :]).astype(sides.dtype)
        boundary_edge_rows = sides.reshape(nrows * 4, sides.shape[2], sides.shape[3])
        edge_add = jnp.einsum(
            "hnu,uqx->hnqx", edge_chooser, boundary_edge_rows, preferred_element_type=jnp.float32
        )
        corner_key = own_csrc * 4 + own_ccode
        corner_select = (corner_key[:, :, None] == slots_range[None, None, :]).astype(corners.dtype)
        corner_rows = corners.reshape(nrows * 4, corners.shape[2])
        corner_increment = jnp.einsum(
            "tek,kc->tec", corner_select, corner_rows, preferred_element_type=jnp.float32
        )
        return (edge_add, corner_increment)

    return picker


def cycle_collector(edge_source, edge_code, corner_source, corner_code, offset_tile, tile_count):
    targets = jnp.arange(tile_count * 4, dtype=jnp.int32)

    def collector(carry, pieces, start):
        sides, corners = pieces
        nrows = sides.shape[0]
        edge_key = ((edge_source - offset_tile) * 4 + edge_code // 2).reshape(nrows * 4)
        edge_chooser = (targets[:, None] == edge_key[None, :]).astype(jnp.float32)
        boundary_edge_rows = sides.reshape(nrows * 4, sides.shape[2] * sides.shape[3])
        edge_add = jnp.dot(
            edge_chooser, boundary_edge_rows, precision=lax.Precision.HIGHEST
        ).reshape(tile_count, 4, sides.shape[2], sides.shape[3])
        corner_key = ((corner_source - offset_tile) * 4 + corner_code).reshape(nrows * 4)
        corner_select = (targets[:, None] == corner_key[None, :]).astype(jnp.float32)
        corner_rows = corners.reshape(nrows * 4, corners.shape[2])
        corner_increment = jnp.dot(
            corner_select, corner_rows, precision=lax.Precision.HIGHEST
        ).reshape(tile_count, 4, corners.shape[2])
        return (carry[0] + edge_add, carry[1] + corner_increment)

    return collector


def local(
    inputs,
    prior_hidden_state,
    cell_prev,
    kernel,
    gate_bias,
    hidden_upstream,
    cell_upstream,
    edge_source,
    edge_code,
    corner_source,
    corner_code,
):
    tile_count, local_ch, pixels = inputs.shape
    offset_tile = lax.axis_index("tile") * tile_count
    own_esrc = lax.dynamic_slice_in_dim(edge_source, offset_tile, tile_count, 0)
    own_ecode = lax.dynamic_slice_in_dim(edge_code, offset_tile, tile_count, 0)
    own_csrc = lax.dynamic_slice_in_dim(corner_source, offset_tile, tile_count, 0)
    own_ccode = lax.dynamic_slice_in_dim(corner_code, offset_tile, tile_count, 0)
    picker = halo_picker(own_esrc, own_ecode, own_csrc, own_ccode)
    full_inputs, full_hidden = (
        lax.all_gather(inputs, "chan", axis=1, tiled=True),
        lax.all_gather(prior_hidden_state, "chan", axis=1, tiled=True),
    )
    tile_field = jnp.concatenate([full_inputs, full_hidden], axis=1).reshape(tile_count, -1, TS, TS)
    feature_channels = tile_field.shape[1]
    start_acc = (
        jnp.zeros((tile_count, 4, feature_channels, TS), jnp.float32),
        jnp.zeros((tile_count, 4, feature_channels), jnp.float32),
    )
    sides, corners = rim_parts(tile_field)
    edge_running_total, corner_acc = picker(
        start_acc,
        (
            lax.all_gather(sides, "tile", axis=0, tiled=True),
            lax.all_gather(corners, "tile", axis=0, tiled=True),
        ),
        jnp.int32(0),
    )
    edges = mirror_edge_order(edge_running_total, own_ecode).astype(jnp.bfloat16)
    padded = assemble(tile_field, edges, corner_acc.astype(jnp.bfloat16))
    feature_channels = padded.shape[1]
    kernels = kernel.reshape(9, 4 * local_ch, feature_channels)
    windows = [
        padded[:, :, offset // 3 : offset // 3 + TS, offset % 3 : offset % 3 + TS].reshape(
            tile_count, feature_channels, pixels
        )
        for offset in range(9)
    ]
    gates = gate_bias.reshape(1, 4 * local_ch, 1)
    for offset in range(9):
        gates = gates + jnp.einsum(
            "gc,ncp->ngp", kernels[offset], windows[offset], preferred_element_type=jnp.float32
        )
    gates = gates.reshape(tile_count, 4, local_ch, pixels)
    in_gate = jax.nn.sigmoid(gates[:, 0])
    forget = jax.nn.sigmoid(gates[:, 1])
    cand = jnp.tanh(gates[:, 2])
    out_gate = jax.nn.sigmoid(gates[:, 3])
    cell_new = forget * cell_prev + in_gate * cand
    squashed = jnp.tanh(cell_new)
    hidden_new = (out_gate * squashed).astype(jnp.bfloat16)
    upstream = hidden_upstream.astype(jnp.float32)
    dcell = cell_upstream + upstream * out_gate * (1.0 - squashed * squashed)
    cell_grad = dcell * forget
    dgates = jnp.stack(
        [
            dcell * cand * in_gate * (1.0 - in_gate),
            dcell * cell_prev * forget * (1.0 - forget),
            dcell * in_gate * (1.0 - cand * cand),
            upstream * squashed * out_gate * (1.0 - out_gate),
        ],
        axis=1,
    )
    dgates = dgates.reshape(tile_count, 4 * local_ch, pixels).astype(jnp.bfloat16)
    bias_local = jnp.sum(dgates.astype(jnp.float32), axis=(0, 2)).reshape(4, local_ch)
    tile_kernel_weight = jnp.stack(
        [
            jnp.einsum("ngp,ncp->gc", dgates, windows[offset], preferred_element_type=jnp.float32)
            for offset in range(9)
        ]
    ).reshape(9, 4, local_ch, feature_channels)
    kernel_grad, bias_grad = lax.psum((tile_kernel_weight, bias_local), "tile")
    dpadded = jnp.zeros((tile_count, feature_channels, TS + 2, TS + 2), jnp.float32)
    for offset in range(9):
        product = jnp.einsum(
            "gc,ngp->ncp", kernels[offset], dgates, preferred_element_type=jnp.float32
        ).reshape(tile_count, feature_channels, TS, TS)
        dpadded = dpadded.at[
            :, :, offset // 3 : offset // 3 + TS, offset % 3 : offset % 3 + TS
        ].add(product)
    chan_count = lax.axis_size("chan")
    shares = lax.psum_scatter(
        dpadded.reshape(tile_count, 2, chan_count, local_ch, (TS + 2) * (TS + 2)),
        "chan",
        scatter_dimension=2,
        tiled=True,
    )
    dlocal = shares.reshape(tile_count, 2 * local_ch, TS + 2, TS + 2)
    cycle_sides, cycle_corners = cycle_parts(dlocal)
    cycle_sides = mirror_edge_order(cycle_sides, own_ecode)
    collector = cycle_collector(
        edge_source, edge_code, corner_source, corner_code, offset_tile, tile_count
    )
    start_sum = (
        jnp.zeros((tile_count, 4, 2 * local_ch, TS), jnp.float32),
        jnp.zeros((tile_count, 4, 2 * local_ch), jnp.float32),
    )
    side_sum, corner_sum = collector(
        start_sum,
        (
            lax.all_gather(cycle_sides.astype(jnp.bfloat16), "tile", axis=0, tiled=True).astype(
                jnp.float32
            ),
            lax.all_gather(cycle_corners.astype(jnp.bfloat16), "tile", axis=0, tiled=True).astype(
                jnp.float32
            ),
        ),
        jnp.int32(0),
    )
    dfield = place_rims(dlocal[:, :, 1:-1, 1:-1], side_sum, corner_sum).reshape(
        tile_count, 2 * local_ch, pixels
    )
    input_grad = dfield[:, :local_ch].astype(jnp.bfloat16)
    hidden_grad = dfield[:, local_ch:].astype(jnp.bfloat16)
    return (hidden_new, cell_new, kernel_grad, bias_grad, input_grad, hidden_grad, cell_grad)


def solution(mesh):
    in_specs = (
        P("tile", "chan", None),
        P("tile", "chan", None),
        P("tile", "chan", None),
        P(None, None, "chan", None),
        P(None, "chan"),
        P("tile", "chan", None),
        P("tile", "chan", None),
        P(),
        P(),
        P(),
        P(),
    )
    out_specs = (
        P("tile", "chan", None),
        P("tile", "chan", None),
        P(None, None, "chan", None),
        P(None, "chan"),
        P("tile", "chan", None),
        P("tile", "chan", None),
        P("tile", "chan", None),
    )
    return jax.shard_map(local, mesh=mesh, in_specs=in_specs, out_specs=out_specs, check_vma=False)
```

profile of v0, /device:TPU:32, one launch (start us, length us, event | category | flops | bytes accessed | tf_op | source)
XLA Modules:
  0.0 1343.3 jit_solution(6722289805705325045)
XLA Ops:
  8.1 7.5 all_gather.18
  16.6 7.4 all_gather.19
  25.1 159.4 %all_gather.20 = bf16[192,4,512]{2,1,0:T(4,128)(2,1)S(1)} all-gather(bf16[3,4,512]{2,1,0:T(4,128)(2,1)S(1)} %copy.173), channel_id=1, replica_groups=mesh['tile'=64,'chan'=4] {'tile'}, dimensions={0}, use_global_device_ids=true | all-gather | bytes 798720 | tf_op jit(solution)/shard_map/all_gather | solution.py:157
  188.2 1.8 fusion.103
  190.0 144.9 %all-gather.3.cloned.1.call-done = bf16[192,4,512,8]{2,3,1,0:T(8,128)(2,1)} async-done(((bf16[3,4,512,8]{2,3,1,0:T(8,128)(2,1)}), bf16[192,4,512,8]{2,3,1,0:T(8,128)(2,1)}) %all-gather.3.cloned.1.call-update) | async-done | bytes 6291472 | tf_op jit(solution)/shard_map/all_gather | solution.py:156
  335.0 6.2 fusion
  345.1 1.9 reshape.944
  346.9 2.9 fusion.104
  350.8 1.7 copy.251
  352.5 1.6 copy.252
  354.1 1.6 copy.253
  355.8 1.9 bitcast_multiply_fusion.4
  361.0 1.8 copy.189
  366.2 1.6 fusion.23
  367.9 2.3 fusion.16
  374.4 1.5 copy.208
  375.9 33.8 %reduce-scatter.2.cloned.1.call-done = f32[3,2,1,64,100]{4,3,1,0,2:T(8,128)} async-done(((f32[3,2,4,64,100]{4,3,1,0,2:T(8,128)}), f32[3,2,1,64,100]{4,3,1,0,2:T(8,128)}) %reduce-scatter.2.cloned.1.call-update) | async-done | bytes 153616 | tf_op jit(solution)/shard_map/reduce_scatter | solution.py:214
  424.7 154.0 %psum.15 = f32[4,64]{1,0:T(4,128)} all-reduce(f32[4,64]{1,0:T(4,128)S(1)} %copy-done.17), channel_id=1, replica_groups=mesh['tile'=64,'chan'=4] {'tile'}, use_global_device_ids=true, to_apply=%region_2.3 | all-reduce | flops 256 | bytes 2048 | tf_op jit(solution)/shard_map/psum | solution.py:204
  579.5 156.0 %all_gather.23 = bf16[192,4,128]{2,1,0:T(4,128)(2,1)S(1)} all-gather(bf16[3,4,128]{2,1,0:T(4,128)(2,1)S(1)} %copy.226), channel_id=1, replica_groups=mesh['tile'=64,'chan'=4] {'tile'}, dimensions={0}, use_global_device_ids=true | all-gather | bytes 199680 | tf_op jit(solution)/shard_map/all_gather | solution.py:236
  735.8 16.5 %copy.219 = bf16[192,4,128,8]{3,2,1,0:T(8,128)(2,1)} copy(bf16[192,4,128,8]{2,3,1,0:T(8,128)(2,1)} %all-gather.5.cloned.1.call-done) | data formatting | bytes 3145728 | tf_op jit(solution)/shard_map/all_gather | solution.py:233
  752.3 36.1 %reshape.960 = bf16[768,1024]{1,0:T(8,128)(2,1)S(1)} reshape(bf16[192,4,128,8]{3,2,1,0:T(8,128)(2,1)} %copy.219) | data formatting | bytes 3145728 | tf_op jit(solution)/shard_map/reshape | solution.py:107
  790.0 1.9 broadcast_select_fusion
  794.8 536.6 %all-reduce.3.cloned.1.call-done = f32[9,4,64,512]{3,2,1,0:T(8,128)} async-done(((f32[9,4,64,512]{3,2,1,0:T(8,128)}), f32[9,4,64,512]{3,2,1,0:T(8,128)}) %all-reduce.3.cloned.1.call-update) | async-done | bytes 4718608 | tf_op jit(solution)/shard_map/psum | solution.py:204
  1331.4 5.4 copy.327
  (186 shorter events, 42.6 us)
Async XLA Ops:
  7.2 180.0 %copy-start.22 = (s32[4]{0:T(128)S(1)}, s32[4]{0:T(128)}, u32[]{:S(2)}) copy-start(s32[4]{0:T(128)} %constant.532.clone.1) | copy-start | bytes 52
  7.2 177.5 %copy-start.14 = (s32[192,4]{0,1:T(4,128)S(1)}, s32[192,4]{0,1:T(4,128)}, u32[]{:S(2)}) copy-start(s32[192,4]{0,1:T(4,128)} %param.54) | copy-start | bytes 9220
  7.2 177.5 %copy-start.15 = (s32[192,4]{0,1:T(4,128)S(1)}, s32[192,4]{0,1:T(4,128)}, u32[]{:S(2)}) copy-start(s32[192,4]{0,1:T(4,128)} %param.55) | copy-start | bytes 9220
  7.2 177.7 %copy-start.16 = (s32[192,4]{0,1:T(4,128)S(1)}, s32[192,4]{0,1:T(4,128)}, u32[]{:S(2)}) copy-start(s32[192,4]{0,1:T(4,128)} %param.52) | copy-start | bytes 9220
  7.2 177.7 %copy-start.13 = (s32[192,4]{0,1:T(4,128)S(1)}, s32[192,4]{0,1:T(4,128)}, u32[]{:S(2)}) copy-start(s32[192,4]{0,1:T(4,128)} %param.53) | copy-start | bytes 9220
  7.2 178.0 %copy-start.20 = (f32[4,64]{1,0:T(4,128)S(1)}, f32[4,64]{1,0:T(4,128)}, u32[]{:S(2)}) copy-start(f32[4,64]{1,0:T(4,128)} %param.49) | copy-start | bytes 3076
  7.2 327.7 %all-gather.3.cloned.1.call-start = ((), (), s32[]{:S(2)}) async-start(), calls=%async_computation.1 | async-start | bytes 6389760 | tf_op jit(solution)/shard_map/all_gather | solution.py:156
  15.7 327.3 %copy-start.2 = (bf16[3,256,64]{1,2,0:T(8,128)(2,1)}, bf16[3,256,64]{1,2,0:T(8,128)(2,1)S(1)}, u32[]{:S(2)}) copy-start(bf16[3,256,64]{1,2,0:T(8,128)(2,1)S(1)} %copy.171) | copy-start | bytes 294916
  25.0 384.7 %reduce-scatter.2.cloned.1.call-start = ((), (), s32[]{:S(2)}) async-start(), calls=%async_computation.3 | async-start | bytes 983040 | tf_op jit(solution)/shard_map/reduce_scatter | solution.py:214
  185.3 156.0 %copy-start.19 = (pred[3,4]{1,0:T(4,128)(4,1)}, pred[3,4]{1,0:T(4,128)(4,1)S(1)}, u32[]{:S(2)}) copy-start(pred[3,4]{1,0:T(4,128)(4,1)S(1)} %copy.174) | copy-start | bytes 40
  335.0 7.1 copy-start.18
  341.2 1.9 copy-start.5
  341.5 2.1 copy-start.11
  350.8 10.2 copy-start
  373.4 42.8 %copy-start.12 = (bf16[3,512,8,1]{1,3,2,0:T(2,128)(2,1)S(1)}, bf16[3,512,8,1]{1,3,2,0:T(2,128)(2,1)}, u32[]{:S(2)}) copy-start(bf16[3,512,8,1]{1,3,2,0:T(2,128)(2,1)} %copy-done.11) | copy-start | bytes 73732
  374.3 43.0 %copy-start.3 = (bf16[3,256,64]{1,2,0:T(8,128)(2,1)S(1)}, bf16[3,256,64]{1,2,0:T(8,128)(2,1)}, u32[]{:S(2)}) copy-start(bf16[3,256,64]{1,2,0:T(8,128)(2,1)} %copy-done.2) | copy-start | bytes 294916
  374.3 43.0 %copy-start.6 = (bf16[3,256,64]{1,2,0:T(8,128)(2,1)S(1)}, bf16[3,256,64]{1,2,0:T(8,128)(2,1)}, u32[]{:S(2)}) copy-start(bf16[3,256,64]{1,2,0:T(8,128)(2,1)} %copy-done.4) | copy-start | bytes 294916
  374.4 44.1 %copy-start.10 = (bf16[3,512,8,1]{1,3,2,0:T(2,128)(2,1)S(1)}, bf16[3,512,8,1]{1,3,2,0:T(2,128)(2,1)}, u32[]{:S(2)}) copy-start(bf16[3,512,8,1]{1,3,2,0:T(2,128)(2,1)} %copy-done.9) | copy-start | bytes 73732
  375.9 359.9 %all-gather.5.cloned.1.call-start = ((), (), s32[]{:S(2)}) async-start(), calls=%async_computation.4 | async-start | bytes 1597440 | tf_op jit(solution)/shard_map/all_gather | solution.py:233
  412.6 918.8 %all-reduce.3.cloned.1.call-start = ((), (), s32[]{:S(2)}) async-start(), calls=%async_computation.2 | async-start | bytes 9437184 | tf_op jit(solution)/shard_map/psum | solution.py:204
  417.3 6.6 copy-start.21
  417.3 7.3 copy-start.17
  417.3 161.3 %copy-start.1 = (f32[3,1,64,64]{3,2,0,1:T(8,128)S(1)}, f32[3,1,64,64]{3,2,0,1:T(8,128)}, u32[]{:S(2)}) copy-start(f32[3,1,64,64]{3,2,0,1:T(8,128)} %copy-done) | copy-start | bytes 147460
  417.3 161.3 %copy-start.8 = (f32[3,64,64]{2,1,0:T(8,128)S(1)}, f32[3,64,64]{2,1,0:T(8,128)}, u32[]{:S(2)}) copy-start(f32[3,64,64]{2,1,0:T(8,128)} %copy-done.7) | copy-start | bytes 147460
  (3 other events, 4.0 us)
Sparse Core Ops, SparseCore 0:
  25.1 309.8 all-gather.2
  376.0 33.6 reduce-scatter.1
  412.7 297.6 all-gather.4
  713.7 617.6 all-reduce.2
where the time goes:
time: 1350 us; the launch traced here: 1340 us
  waiting for transfers between devices  715 us (53%)
  blocking collectives  484 us (36%)
  local copies, waits for them, and re-layouts  87.7 us (6%)
  matrix products  21.7 us (2%)
  other arithmetic  19.5 us (1%)
  between operations  14.7 us (1%)
    psum x1, waiting for transfers between devices, local(): kernel_grad, bias_grad = lax.psum((tile_kernel_weight, bias_local), 'tile')  537 us
    all_gather x1, blocking collectives, local(): lax.all_gather(corners, 'tile', axis=0, tiled=True)  159 us
    all_gather x1, blocking collectives, local(): lax.all_gather(cycle_corners.astype(jnp.bfloat16), 'tile', axis=0, tiled=...  156 us
    psum x1, blocking collectives, local(): kernel_grad, bias_grad = lax.psum((tile_kernel_weight, bias_local), 'tile')  154 us
    all_gather x1, waiting for transfers between devices, local(): lax.all_gather(sides, 'tile', axis=0, tiled=True)  145 us
    reshape x1, local copies, waits for them, and re-layouts, collector(): sides.reshape(nrows * 4, sides.shape[2] * sides.shape[3])  36.1 us
    reduce_scatter x1, waiting for transfers between devices, local(): lax.psum_scatter(dpadded.reshape(tile_count, 2, chan_count, local_ch, (TS...  33.8 us
  transfers between devices with their start and end apart: 4, of which 3 were waited for; matrix products, arithmetic and copies ran while one was open for 6% of the time, Pallas kernels for 0%

commit v1 on v0

v1 whole, which is shorter than its diff:
```python
import functools

import jax
import jax.numpy as jnp
from jax import lax
from jax.experimental import pallas as pl
from jax.experimental.pallas import tpu as pltpu
from jax.sharding import PartitionSpec as P

F32, BF16, I32 = jnp.float32, jnp.bfloat16, jnp.int32
MESH = pl.DeviceIdType.MESH
NY, NX, NZ = 2, 4, 8
NQ = NY * NX
NC = 4
TPD = 3
PIX = 64
RIM = 32 * TPD
MARGIN = 112
BODY = 80 * TPD
DROWS = BODY + 64
UNIT = 1024
JOBS = ((0, 2, "zxy"), (2, 3, "xyz"), (5, 4, "yxz"))
VMEM_LIMIT = 56 * 1024 * 1024


def nn(a, b):
    return lax.dot_general(a, b, (((1,), (0,)), ((), ())), preferred_element_type=F32)


def nt(a, b):
    return lax.dot_general(a, b, (((1,), (1,)), ((), ())), preferred_element_type=F32)


def iota(shape, dim):
    return lax.broadcasted_iota(I32, shape, dim)


def eye(n):
    return (iota((n, n), 0) == iota((n, n), 1)).astype(BF16)


def position():
    t = lax.axis_index("tile")
    z, q = lax.rem(t, NZ), lax.div(t, NZ)
    return q, lax.div(q, NX), lax.rem(q, NX), z, lax.axis_index("chan")


def peers():
    q, y, x, z, c = position()
    return {
        "z": lambda d: (q * NZ + lax.rem(z + d, NZ), c),
        "q": lambda d: (lax.rem(q + d, NQ) * NZ + z, c),
        "x": lambda d: ((y * NX + lax.rem(x + d, NX)) * NZ + z, c),
        "y": lambda d: ((lax.rem(y + d, NY) * NX + x) * NZ + z, c),
        "c": lambda d: (q * NZ + z, lax.rem(c + d, NC)),
    }


def entry_barrier(to):
    barrier = pltpu.get_barrier_semaphore()
    count = 0
    for axis, size in (("z", NZ), ("q", NQ), ("c", NC)):
        for d in range(1, size):
            pl.semaphore_signal(barrier, inc=1, device_id=to[axis](d), device_id_type=MESH)
            count += 1
    pl.semaphore_wait(barrier, count)


def send(src, dst, send_sem, recv_sem, device):
    pltpu.make_async_remote_copy(
        src_ref=src,
        dst_ref=dst,
        send_sem=send_sem,
        recv_sem=recv_sem,
        device_id=device,
        device_id_type=MESH,
    ).start()


def await_bytes(like, sem):
    pltpu.make_async_copy(like, like, sem).wait()


def prepare_kernel(
    inp, hid, esrc, ecode, csrc, ccode, field_out, rim_out, index_out, cells, index
):
    ident = eye(PIX)
    for t in range(TPD):
        both = jnp.concatenate([inp[t], hid[t]], axis=0)
        cells[t * PIX : (t + 1) * PIX, :] = nt(ident, both)
    field_out[...] = cells[...].astype(BF16)
    for t in range(TPD):
        base = t * PIX
        rim = jnp.concatenate(
            [
                cells[base : base + 8, :],
                cells[pl.ds(base + 7, 8, stride=8), :],
                cells[base + 56 : base + 64, :],
                cells[pl.ds(base, 8, stride=8), :],
            ],
            axis=0,
        )
        rim_out[t * 32 : (t + 1) * 32, :] = rim.astype(BF16)
    lane, row = iota((4, 128), 1), iota((4, 128), 0)
    edge_lane = ((lane < 32) & (lax.div(lane, 8) == row)).astype(BF16)
    corner_lane = (lane - 32 == row).astype(BF16)

    def spread(edges, corners):
        wide = nn(edges[...].astype(F32).astype(BF16), edge_lane)
        wide += nn(corners[...].astype(F32).astype(BF16), corner_lane)
        return wide.astype(I32)

    source, code = spread(esrc, csrc), spread(ecode, ccode)
    lane = iota(source.shape, 1)
    cell = lane & 7
    along_side = (code >> 1) * 8 + jnp.where((code & 1) == 1, 7 - cell, cell)
    at_corner = jnp.where(
        code == 0, 0, jnp.where(code == 1, 7, jnp.where(code == 2, 23, 16))
    )
    index[...] = source * 32 + jnp.where(lane < 32, along_side, at_corner)
    devices = index_out.shape[0]
    rows = [index[pl.ds(i, devices, stride=TPD), :] for i in range(TPD)]
    index_out[...] = jnp.concatenate(
        [r[:, :32] for r in rows]
        + [r[:, 32:36] for r in rows]
        + [jnp.full((devices, 128 - 36 * TPD), -1000000, I32)],
        axis=1,
    )


def prepare(inp, hid, esrc, ecode, csrc, ccode):
    devices = NQ * NZ
    vmem = pl.BlockSpec(memory_space=pltpu.VMEM)
    return pl.pallas_call(
        prepare_kernel,
        out_shape=(
            jax.ShapeDtypeStruct((TPD * PIX, 128), BF16),
            jax.ShapeDtypeStruct((RIM, 128), BF16),
            jax.ShapeDtypeStruct((devices, 128), I32),
        ),
        in_specs=[vmem] * 6,
        out_specs=(vmem,) * 3,
        scratch_shapes=[
            pltpu.VMEM((TPD * PIX, 128), F32),
            pltpu.VMEM((devices * TPD, 128), I32),
        ],
        name="prepare",
    )(inp, hid, esrc, ecode, csrc, ccode)


def halo_kernel(
    rim, field, index, field_all, margin_all, table, picked, arrived, sems_s, sems_r
):
    q, y, x, z, c = position()
    to = peers()
    entry_barrier(to)
    for d in range(1, NZ):
        send(rim, table.at[z], sems_s.at[0], sems_r.at[0], to["z"](d))
    for d in range(1, NC):
        send(field, field_all.at[c], sems_s.at[1], sems_r.at[1], to["c"](d))
    table[z] = rim[...]
    field_all[c] = field[...]

    first = q * (NZ * RIM)
    choosers = []
    for d in range(NQ):
        row = index[pl.ds(lax.rem(q + d, NQ) * NZ + z, 1), :]
        down = jnp.broadcast_to((row - first).astype(F32), (128, 128)).T
        choosers.append(
            jnp.concatenate(
                [
                    (down == (iota((128, 128), 1) + 128 * k).astype(F32)).astype(BF16)
                    for k in range(NZ * RIM // 128)
                ],
                axis=1,
            )
        )
    await_bytes(table.at[pl.ds(0, NZ - 1)], sems_r.at[0])
    cells = table[...].reshape(NZ * RIM, 128)
    for d in range(NQ):
        picked[d] = nn(choosers[d], cells)[:MARGIN].astype(BF16)
        if d:
            send(picked.at[d], arrived.at[d - 1], sems_s.at[2], sems_r.at[2], to["q"](d))
    await_bytes(arrived, sems_r.at[2])
    total = picked[0].astype(F32)
    for d in range(1, NQ):
        total += arrived[d - 1].astype(F32)
    margin_all[c] = total.astype(BF16)
    for d in range(1, NC):
        send(margin_all.at[c], margin_all.at[c], sems_s.at[3], sems_r.at[3], to["c"](d))
    await_bytes(field_all.at[pl.ds(0, NC - 1)], sems_r.at[1])
    await_bytes(margin_all.at[pl.ds(0, NC - 1)], sems_r.at[3])
    await_bytes(table.at[pl.ds(0, NZ - 1)], sems_s.at[0])
    await_bytes(field_all.at[pl.ds(0, NC - 1)], sems_s.at[1])
    await_bytes(arrived, sems_s.at[2])
    await_bytes(margin_all.at[pl.ds(0, NC - 1)], sems_s.at[3])


def halo(rim, field, index):
    vmem = pl.BlockSpec(memory_space=pltpu.VMEM)
    return pl.pallas_call(
        halo_kernel,
        out_shape=(
            jax.ShapeDtypeStruct((NC, TPD * PIX, 128), BF16),
            jax.ShapeDtypeStruct((NC, MARGIN, 128), BF16),
        ),
        in_specs=[vmem] * 3,
        out_specs=(vmem,) * 2,
        scratch_shapes=[
            pltpu.VMEM((NZ, RIM, 128), BF16),
            pltpu.VMEM((NQ, MARGIN, 128), BF16),
            pltpu.VMEM((NQ - 1, MARGIN, 128), BF16),
            pltpu.SemaphoreType.DMA((4,)),
            pltpu.SemaphoreType.DMA((4,)),
        ],
        compiler_params=pltpu.CompilerParams(
            collective_id=0, has_side_effects=True, vmem_limit_bytes=VMEM_LIMIT
        ),
        name="halo",
    )(rim, field, index)


def step_kernel(
    field_all,
    margin_all,
    kern,
    bias,
    cell_prev,
    cell_up,
    hidden_up,
    hidden_out,
    cell_out,
    cell_grad_out,
    grad_out,
    bias_out,
    dpad_out,
    wide,
    windows,
    accs,
):
    for k in range(4):
        pair, half = 2 * (k % 2), 64 * (k // 2)

        def lanes(ref):
            return jnp.concatenate(
                [ref[pair][:, half : half + 64], ref[pair + 1][:, half : half + 64]], axis=1
            ).astype(F32)

        body, margin = lanes(field_all), lanes(margin_all)
        for t in range(TPD):
            base, rim = t * 80, t * 32
            wide[1, k, base : base + 8, :] = margin[rim : rim + 8]
            wide[1, k, base + 8 : base + 72, :] = body[t * PIX : (t + 1) * PIX]
            wide[1, k, base + 72 : base + 80, :] = margin[rim + 16 : rim + 24]
        wide[0, k, 1:BODY, :] = wide[1, k, 0 : BODY - 1, :]
        wide[2, k, 0 : BODY - 1, :] = wide[1, k, 1:BODY, :]
        for t in range(TPD):
            base, rim, corner = t * 80, t * 32, RIM + t * 4
            left, right = wide.at[0, k], wide.at[2, k]
            left[base : base + 1, :] = margin[corner : corner + 1]
            left[pl.ds(base + 8, 8, stride=8), :] = margin[rim + 24 : rim + 32]
            left[base + 72 : base + 73, :] = margin[corner + 3 : corner + 4]
            right[base + 7 : base + 8, :] = margin[corner + 1 : corner + 2]
            right[pl.ds(base + 15, 8, stride=8), :] = margin[rim + 8 : rim + 16]
            right[base + 79 : base + 80, :] = margin[corner + 2 : corner + 3]
    for o in range(9):
        a, b = o // 3, o % 3
        for k in range(4):
            for t in range(TPD):
                base = t * 80 + a * 8
                windows[o, t * PIX : (t + 1) * PIX, k * 128 : (k + 1) * 128] = wide[
                    b, k, base : base + PIX, :
                ].astype(BF16)

    gates = bias[...] + nt(kern[0], windows[0])
    for o in range(1, 9):
        gates = gates + nt(kern[o], windows[o])
    in_gate = jax.nn.sigmoid(gates[0:64])
    forget = jax.nn.sigmoid(gates[64:128])
    cand = jnp.tanh(gates[128:192])
    out_gate = jax.nn.sigmoid(gates[192:256])
    before = jnp.concatenate([cell_prev[t] for t in range(TPD)], axis=1)
    above = jnp.concatenate([cell_up[t] for t in range(TPD)], axis=1)
    upstream = jnp.concatenate([hidden_up[t].astype(F32) for t in range(TPD)], axis=1)
    cell_new = forget * before + in_gate * cand
    squashed = jnp.tanh(cell_new)
    hidden_new = (out_gate * squashed).astype(BF16)
    dcell = above + upstream * out_gate * (1.0 - squashed * squashed)
    cell_grad = dcell * forget
    for t in range(TPD):
        at = slice(t * PIX, (t + 1) * PIX)
        hidden_out[t] = hidden_new[:, at]
        cell_out[t] = cell_new[:, at]
        cell_grad_out[t] = cell_grad[:, at]
    dgates = jnp.concatenate(
        [
            dcell * cand * in_gate * (1.0 - in_gate),
            dcell * before * forget * (1.0 - forget),
            dcell * in_gate * (1.0 - cand * cand),
            upstream * squashed * out_gate * (1.0 - out_gate),
        ],
        axis=0,
    ).astype(BF16)
    bias_out[...] = nt(jnp.ones((8, TPD * PIX), BF16), dgates)
    for o in range(9):
        grad = nn(dgates, windows[o]).astype(BF16)
        for k in range(4):
            grad_out[o, k] = grad[:, k * 128 : (k + 1) * 128]
    turned = nt(eye(TPD * PIX), dgates).astype(BF16)
    accs[...] = jnp.zeros(accs.shape, F32)
    for o in range(9):
        a, b = o // 3, o % 3
        product = nn(turned, kern[o])
        for k in range(4):
            for t in range(TPD):
                base = 8 + t * 80 + a * 8
                accs[b, k, base : base + PIX, :] += product[
                    t * PIX : (t + 1) * PIX, k * 128 : (k + 1) * 128
                ]
    column = iota((BODY, 128), 0) & 7
    blocks = []
    for k in range(4):
        body = accs[1, k, 8 : 8 + BODY, :]
        body += jnp.where(column < 7, accs[0, k, 9 : 9 + BODY, :], 0.0)
        body += jnp.where(column > 0, accs[2, k, 7 : 7 + BODY, :], 0.0)
        left, right = accs.at[0, k], accs.at[2, k]
        blocks.append(
            (
                body,
                left[pl.ds(8, 32, stride=8), :],
                right[pl.ds(15, 32, stride=8), :],
            )
        )
    for c in range(NC):
        half = slice((c % 2) * 64, (c % 2) * 64 + 64)
        low, high = blocks[c // 2], blocks[2 + c // 2]
        start = 0
        for one, two in zip(low, high):
            rows = one.shape[0]
            dpad_out[c, start : start + rows, :] = jnp.concatenate(
                [one[:, half], two[:, half]], axis=1
            ).astype(BF16)
            start += rows


def step(field_all, margin_all, kern, bias, cell_prev, cell_up, hidden_up):
    vmem = pl.BlockSpec(memory_space=pltpu.VMEM)
    state = cell_prev.shape
    return pl.pallas_call(
        step_kernel,
        out_shape=(
            jax.ShapeDtypeStruct(state, BF16),
            jax.ShapeDtypeStruct(state, F32),
            jax.ShapeDtypeStruct(state, F32),
            jax.ShapeDtypeStruct((9, 4, 256, 128), BF16),
            jax.ShapeDtypeStruct((8, 256), F32),
            jax.ShapeDtypeStruct((NC, DROWS, 128), BF16),
        ),
        in_specs=[vmem] * 7,
        out_specs=(vmem,) * 6,
        scratch_shapes=[
            pltpu.VMEM((3, 4, BODY, 128), F32),
            pltpu.VMEM((9, TPD * PIX, 512), BF16),
            pltpu.VMEM((3, 4, 8 + BODY + 32, 128), F32),
        ],
        compiler_params=pltpu.CompilerParams(vmem_limit_bytes=VMEM_LIMIT),
        name="step",
    )(field_all, margin_all, kern, bias, cell_prev, cell_up, hidden_up)


def axis_size(axis):
    return {"x": NX, "y": NY, "z": NZ}[axis]


def reduce_kernel(
    grad,
    bias,
    dpad,
    index,
    grad_out,
    bias_out,
    inner_out,
    side_out,
    dpad_in,
    dsum,
    margin_own,
    margin_send,
    margin_in,
    slot_sum,
    slot_send,
    slot_in,
    bias_in_q,
    bias_mid,
    bias_in_z,
    *rest,
):
    jobs = len(JOBS)
    landing = [rest[5 * j : 5 * j + 3] for j in range(jobs)]
    passing = [rest[5 * j + 3 : 5 * j + 5] for j in range(jobs)]
    small_s, small_r, job_s, job_r = rest[5 * jobs :]
    q, y, x, z, c = position()
    here = {"x": x, "y": y, "z": z}
    to = peers()

    def rows_of(j, stage):
        rows = JOBS[j][1] * UNIT
        for axis in JOBS[j][2][:stage]:
            rows //= axis_size(axis)
        return rows

    def start_of(j, stage):
        first = JOBS[j][0] * UNIT
        rows = JOBS[j][1] * UNIT
        for axis in JOBS[j][2][:stage]:
            rows //= axis_size(axis)
            first = first + here[axis] * rows
        return pl.multiple_of(first, 16) if stage else first

    def scatter(j, stage):
        axis = JOBS[j][2][stage]
        size, rows = axis_size(axis), rows_of(j, stage + 1)
        for d in range(1, size):
            chunk = lax.rem(here[axis] + d, size) * rows
            if stage == 0:
                src = grad.at[pl.ds(pl.multiple_of(JOBS[j][0] * UNIT + chunk, 16), rows)]
            else:
                src = passing[j][stage - 1].at[pl.ds(pl.multiple_of(chunk, 16), rows)]
            send(
                src,
                landing[j][stage].at[d - 1],
                job_s.at[j, stage],
                job_r.at[j, stage],
                to[axis](d),
            )

    def gather(j, stage):
        axis = JOBS[j][2][stage]
        size, rows = axis_size(axis), rows_of(j, stage + 1)
        mine = grad_out.at[pl.ds(start_of(j, stage + 1), rows)]
        for d in range(1, size):
            send(mine, mine, job_s.at[j, 3 + stage], job_r.at[j, 3 + stage], to[axis](d))

    def add_up(j, stage):
        axis = JOBS[j][2][stage]
        rows = rows_of(j, stage + 1)
        await_bytes(landing[j][stage], job_r.at[j, stage])
        mine = here[axis] * rows
        block = min(rows, 128)
        while rows % block:
            block -= 16

        def one(i, carry):
            at = pl.multiple_of(i * block, 16)
            if stage == 0:
                from_row = pl.multiple_of(JOBS[j][0] * UNIT + mine + at, 16)
                total = grad[pl.ds(from_row, block), :].astype(F32)
            else:
                from_row = pl.multiple_of(mine + at, 16)
                total = passing[j][stage - 1][pl.ds(from_row, block), :].astype(F32)
            for d in range(axis_size(axis) - 1):
                total += landing[j][stage][d, pl.ds(at, block), :].astype(F32)
            if stage < 2:
                passing[j][stage][pl.ds(at, block), :] = total.astype(BF16)
            else:
                into = pl.multiple_of(start_of(j, 3) + at, 16)
                grad_out[pl.ds(into, block), :] = total.astype(BF16)
            return carry

        if rows == block:
            one(0, 0)
        else:
            lax.fori_loop(0, rows // block, one, 0)

    def gathered(j, stage):
        axis = JOBS[j][2][stage]
        rows = rows_of(j, stage + 1) * (axis_size(axis) - 1)
        await_bytes(grad_out.at[pl.ds(0, rows)], job_r.at[j, 3 + stage])

    entry_barrier(to)
    for d in range(1, NC):
        send(
            dpad.at[lax.rem(c + d, NC)],
            dpad_in.at[d - 1],
            small_s.at[0],
            small_r.at[0],
            to["c"](d),
        )
    for j in range(jobs):
        scatter(j, 0)
    for d in range(1, NQ):
        send(bias, bias_in_q.at[d - 1], small_s.at[1], small_r.at[1], to["q"](d))

    await_bytes(dpad_in, small_r.at[0])
    total = dpad[c].astype(F32)
    for d in range(NC - 1):
        total += dpad_in[d].astype(F32)
    dsum[...] = total
    left, right = BODY, BODY + 32
    margin_own[...] = jnp.zeros(margin_own.shape, F32)
    for t in range(TPD):
        base, rim, corner, col = t * 80, t * 32, RIM + t * 4, t * 10
        margin_own[rim : rim + 8, :] = dsum[base : base + 8, :]
        margin_own[rim + 8 : rim + 16, :] = dsum[right + col + 1 : right + col + 9, :]
        margin_own[rim + 16 : rim + 24, :] = dsum[base + 72 : base + 80, :]
        margin_own[rim + 24 : rim + 32, :] = dsum[left + col + 1 : left + col + 9, :]
        margin_own[corner : corner + 1, :] = dsum[left + col : left + col + 1, :]
        margin_own[corner + 1 : corner + 2, :] = dsum[right + col : right + col + 1, :]
        margin_own[corner + 2 : corner + 3, :] = dsum[right + col + 9 : right + col + 10, :]
        margin_own[corner + 3 : corner + 4, :] = dsum[left + col + 9 : left + col + 10, :]
        inner_out[t * PIX : (t + 1) * PIX, :] = dsum[base + 8 : base + 72, :]
    margin_send[...] = margin_own[...].astype(BF16)
    for d in range(1, NQ):
        send(margin_send, margin_in.at[d - 1], small_s.at[2], small_r.at[2], to["q"](d))

    for j in range(jobs):
        add_up(j, 0)
        scatter(j, 1)

    first = q * (NZ * RIM)
    choosers = []
    for d in range(NQ):
        row = index[pl.ds(lax.rem(q + NQ - d, NQ) * NZ + z, 1), :][:, :MARGIN]
        chooser = (iota((NZ * RIM, MARGIN), 0) == row - first).astype(F32).astype(BF16)
        choosers.append(chooser)
    await_bytes(margin_in, small_r.at[2])
    sums = nn(choosers[0], margin_send[...])
    for d in range(1, NQ):
        sums += nn(choosers[d], margin_in[d - 1])
    slot_sum[...] = sums.reshape(NZ, RIM, 128)
    slot_send[...] = slot_sum[...].astype(BF16)
    for d in range(1, NZ):
        send(
            slot_send.at[lax.rem(z + d, NZ)],
            slot_in.at[d - 1],
            small_s.at[3],
            small_r.at[3],
            to["z"](d),
        )
    await_bytes(bias_in_q, small_r.at[1])
    total = bias[...]
    for d in range(NQ - 1):
        total += bias_in_q[d]
    bias_mid[...] = total
    for d in range(1, NZ):
        send(bias_mid, bias_in_z.at[d - 1], small_s.at[4], small_r.at[4], to["z"](d))

    for j in range(jobs):
        add_up(j, 1)
        scatter(j, 2)

    await_bytes(slot_in, small_r.at[3])
    total = slot_sum[z]
    for d in range(NZ - 1):
        total += slot_in[d].astype(F32)
    side_out[...] = total
    await_bytes(bias_in_z, small_r.at[4])
    total = bias_mid[...]
    for d in range(NZ - 1):
        total += bias_in_z[d]
    bias_out[...] = total

    for j in range(jobs):
        add_up(j, 2)
        gather(j, 2)
    for stage in (2, 1):
        for j in range(jobs):
            gathered(j, stage)
            gather(j, stage - 1)
    for j in range(jobs):
        gathered(j, 0)

    await_bytes(dpad_in, small_s.at[0])
    await_bytes(bias_in_q, small_s.at[1])
    await_bytes(margin_in, small_s.at[2])
    await_bytes(slot_in, small_s.at[3])
    await_bytes(bias_in_z, small_s.at[4])
    for j in range(jobs):
        for stage in range(3):
            await_bytes(landing[j][stage], job_s.at[j, stage])
            axis = JOBS[j][2][stage]
            rows = rows_of(j, stage + 1) * (axis_size(axis) - 1)
            await_bytes(grad_out.at[pl.ds(0, rows)], job_s.at[j, 3 + stage])


def reduce_all(grad, bias, dpad, index):
    vmem = pl.BlockSpec(memory_space=pltpu.VMEM)
    scratch = [
        pltpu.VMEM((NC - 1, DROWS, 128), BF16),
        pltpu.VMEM((DROWS, 128), F32),
        pltpu.VMEM((MARGIN, 128), F32),
        pltpu.VMEM((MARGIN, 128), BF16),
        pltpu.VMEM((NQ - 1, MARGIN, 128), BF16),
        pltpu.VMEM((NZ, RIM, 128), F32),
        pltpu.VMEM((NZ, RIM, 128), BF16),
        pltpu.VMEM((NZ - 1, RIM, 128), BF16),
        pltpu.VMEM((NQ - 1, 8, 256), F32),
        pltpu.VMEM((8, 256), F32),
        pltpu.VMEM((NZ - 1, 8, 256), F32),
    ]
    for _, units, order in JOBS:
        rows, held = units * UNIT, []
        for axis in order:
            size = axis_size(axis)
            rows //= size
            scratch.append(pltpu.VMEM((size - 1, rows, 128), BF16))
            held.append(pltpu.VMEM((rows, 128), BF16))
        scratch += held[:2]
    scratch += [
        pltpu.SemaphoreType.DMA((5,)),
        pltpu.SemaphoreType.DMA((5,)),
        pltpu.SemaphoreType.DMA((len(JOBS), 6)),
        pltpu.SemaphoreType.DMA((len(JOBS), 6)),
    ]
    return pl.pallas_call(
        reduce_kernel,
        out_shape=(
            jax.ShapeDtypeStruct((9 * UNIT, 128), BF16),
            jax.ShapeDtypeStruct((8, 256), F32),
            jax.ShapeDtypeStruct((TPD * PIX, 128), F32),
            jax.ShapeDtypeStruct((RIM, 128), F32),
        ),
        in_specs=[vmem] * 4,
        out_specs=(vmem,) * 4,
        scratch_shapes=scratch,
        compiler_params=pltpu.CompilerParams(
            collective_id=1, has_side_effects=True, vmem_limit_bytes=VMEM_LIMIT
        ),
        name="reduce_all",
    )(grad, bias, dpad, index)


def finish_kernel(grad, inner, sides, grad_out, input_out, hidden_out, cells):
    for k in range(4):
        grad_out[0, :, k * 128 : (k + 1) * 128] = grad[0, k].astype(F32)

    @pl.when(pl.program_id(0) == 0)
    def _():
        cells[...] = inner[...]
        for t in range(TPD):
            base, rim = t * PIX, t * 32
            cells[base : base + 8, :] += sides[rim : rim + 8, :]
            cells[pl.ds(base + 7, 8, stride=8), :] += sides[rim + 8 : rim + 16, :]
            cells[base + 56 : base + 64, :] += sides[rim + 16 : rim + 24, :]
            cells[pl.ds(base, 8, stride=8), :] += sides[rim + 24 : rim + 32, :]
        ident = eye(128)
        for t in range(TPD):
            rounded = cells[t * PIX : (t + 1) * PIX, :].astype(BF16)
            turned = nt(ident, rounded).astype(BF16)
            input_out[t] = turned[0:64]
            hidden_out[t] = turned[64:128]


def finish(grad, inner, sides):
    whole = lambda shape: pl.BlockSpec(shape, lambda i: (0,) * len(shape))
    state = jax.ShapeDtypeStruct((TPD, 64, PIX), BF16)
    return pl.pallas_call(
        finish_kernel,
        grid=(9,),
        out_shape=(jax.ShapeDtypeStruct((9, 256, 512), F32), state, state),
        in_specs=[
            pl.BlockSpec((1, 4, 256, 128), lambda i: (i, 0, 0, 0)),
            whole(inner.shape),
            whole(sides.shape),
        ],
        out_specs=(
            pl.BlockSpec((1, 256, 512), lambda i: (i, 0, 0)),
            whole(state.shape),
            whole(state.shape),
        ),
        scratch_shapes=[pltpu.VMEM((TPD * PIX, 128), F32)],
        name="finish",
    )(grad, inner, sides)


def local(
    inputs,
    prior_hidden_state,
    cell_prev,
    kernel,
    gate_bias,
    hidden_upstream,
    cell_upstream,
    edge_source,
    edge_code,
    corner_source,
    corner_code,
):
    field, rim, index = prepare(
        inputs, prior_hidden_state, edge_source, edge_code, corner_source, corner_code
    )
    field_all, margin_all = halo(rim, field, index)
    hidden_new, cell_new, cell_grad, grad, bias, dpad = step(
        field_all,
        margin_all,
        kernel.reshape(9, 256, 512),
        gate_bias.reshape(256, 1),
        cell_prev,
        cell_upstream,
        hidden_upstream,
    )
    grad, bias, inner, sides = reduce_all(grad.reshape(9 * UNIT, 128), bias, dpad, index)
    kernel_grad, input_grad, hidden_grad = finish(grad.reshape(9, 4, 256, 128), inner, sides)
    return (
        hidden_new,
        cell_new,
        kernel_grad.reshape(9, 4, 64, 512),
        bias[0].reshape(4, 64),
        input_grad,
        hidden_grad,
        cell_grad,
    )


def solution(mesh):
    tiles, whole = P("tile", "chan", None), P()
    gates = P(None, None, "chan", None)
    bias = P(None, "chan")
    in_specs = (tiles, tiles, tiles, gates, bias, tiles, tiles, whole, whole, whole, whole)
    out_specs = (tiles, tiles, gates, bias, tiles, tiles, tiles)
    return jax.shard_map(local, mesh=mesh, in_specs=in_specs, out_specs=out_specs, check_vma=False)
```

time: 1350 us -> 115 us (0.09)
  waiting for transfers between devices: 715 us -> 0 us
  blocking collectives: 484 us -> 0 us
  Pallas kernels: 0 us -> 105 us
  local copies, waits for them, and re-layouts: 87.7 us -> 8.63 us
  matrix products: 21.7 us -> 0 us
  other arithmetic: 19.5 us -> 0 us
  between operations: 14.7 us -> 0.65 us
    psum x1 -> x0, waiting for transfers between devices: 537 us -> none  [local(): kernel_grad, bias_grad = lax.psum((tile_kernel_weight, bias_local), 'tile')]
    all_gather x4 -> x0, blocking collectives: 330 us -> none  [the longest x1 159 us: local(): lax.all_gather(corners, 'tile', axis=0, tiled=True)]
    psum x1 -> x0, blocking collectives: 154 us -> none  [local(): kernel_grad, bias_grad = lax.psum((tile_kernel_weight, bias_local), 'tile')]
    all_gather x2 -> x0, waiting for transfers between devices: 145 us -> none  [the longest x1 145 us: local(): lax.all_gather(sides, 'tile', axis=0, tiled=True)]
    pallas_call x0 -> x5, Pallas kernels: none -> 105 us  [the longest x1 64.9 us: reduce_all(): pl.pallas_call(reduce_kernel, out_shape=(jax.ShapeDtypeStruct((9 * UNIT,...]
    reshape x6 -> x1, local copies, waits for them, and re-layouts: 40.7 us -> 1.47 us  [local(): gate_bias.reshape(256, 1)]
    reduce_scatter x1 -> x0, waiting for transfers between devices: 33.8 us -> none  [local(): lax.psum_scatter(dpadded.reshape(tile_count, 2, chan_count, local_ch, (TS...]
    dot_general x31 -> x0, matrix products: 21.7 us -> none  [the longest x9 9.65 us: local(): jnp.einsum('ngp,ncp->gc', dgates, windows[offset], preferred_element_type...]
  transfers between devices with their start and end apart: 4 -> 0, of which waited for: 3 -> 0; matrix products, arithmetic and copies ran while one was open for 6% -> 0% of each run, Pallas kernels for 0% -> 0%
where the time goes in v1:
time: 115 us
  Pallas kernels  105 us (91%)
  local copies, waits for them, and re-layouts  8.63 us (8%)
    pallas_call x1, Pallas kernels, reduce_all(): pl.pallas_call(reduce_kernel, out_shape=(jax.ShapeDtypeStruct((9 * UNIT,...  64.9 us
    pallas_call x1, Pallas kernels, halo(): pl.pallas_call(halo_kernel, out_shape=(jax.ShapeDtypeStruct((NC, TPD * PI...  24.9 us
    pallas_call x1, Pallas kernels, finish(): pl.pallas_call(finish_kernel, grid=(9,), out_shape=(jax.ShapeDtypeStruct(...  7 us
    pallas_call x1, Pallas kernels, step(): pl.pallas_call(step_kernel, out_shape=(jax.ShapeDtypeStruct(state, BF16),...  6.64 us
    unnamed x4, local copies, waits for them, and re-layouts  5.78 us

profile of v1, /device:TPU:32, one launch (start us, length us, event | category | flops | bytes accessed | tf_op | source)
XLA Modules:
  0.0 114.7 jit_solution(990190171742474048)
XLA Ops:
  0.6 1.4 %copy.22.esrc = s32[192,4]{1,0:T(8,128)} copy(s32[192,4]{0,1:T(4,128)} %param.18) | data formatting | bytes 6144 | tf_op args[7]
  2.1 1.4 %copy.23.ecode = s32[192,4]{1,0:T(8,128)} copy(s32[192,4]{0,1:T(4,128)} %param.19) | data formatting | bytes 6144 | tf_op args[8]
  3.5 1.4 %copy.24.csrc = s32[192,4]{1,0:T(8,128)} copy(s32[192,4]{0,1:T(4,128)} %param.20) | data formatting | bytes 6144 | tf_op args[9]
  5.0 1.4 %copy.25.ccode = s32[192,4]{1,0:T(8,128)} copy(s32[192,4]{0,1:T(4,128)} %param.21) | data formatting | bytes 6144 | tf_op args[10]
  6.4 2.1 %prepare.1 = (bf16[192,128]{1,0:T(8,128)(2,1)}, bf16[96,128]{1,0:T(8,128)(2,1)}, s32[64,128]{1,0:T(8,128)}) custom-call(bf16[3,64,64]{2,1,0:T(8,128)(2,1)} %inp.1, bf16[3,64,64]{2,1,0:T(8,128)(2,1)} %hid.1, s32[192,4]{1,0:T(8,128)} %copy.22.esrc, s32[192,4]{1,0:T(8,128)} %copy.23.ecode, s32[192,4]{1,0:T(8,128)} %copy.24.csrc, s32[192,4]{1,0:T(8,128)} %copy.25.ccode), custom_call_target="tpu_custom_call" | custom-call | tf_op jit(solution)/shard_map/prepare/pallas_call | solution.py:134
  8.5 1.5 %reshape.34.bias = f32[256,1]{1,0:T(8,128)} reshape(f32[4,64]{1,0:T(4,128)} %param.15) | data formatting | bytes 2048 | tf_op jit(solution)/shard_map/reshape | solution.py:696
  10.0 24.9 %halo.1 = (bf16[4,192,128]{2,1,0:T(8,128)(2,1)}, bf16[4,112,128]{2,1,0:T(8,128)(2,1)}) custom-call(bf16[96,128]{1,0:T(8,128)(2,1)} %get-tuple-element.25.rim, bf16[192,128]{1,0:T(8,128)(2,1)} %get-tuple-element.26.field, s32[64,128]{1,0:T(8,128)} %get-tuple-element.27.index), custom_call_target="tpu_custom_call" | custom-call | tf_op jit(solution)/shard_map/halo/pallas_call | solution.py:201
  34.8 6.6 %step.1 = (bf16[3,64,64]{2,1,0:T(8,128)(2,1)}, f32[3,64,64]{2,1,0:T(8,128)}, f32[3,64,64]{2,1,0:T(8,128)}, bf16[9,4,256,128]{3,2,1,0:T(8,128)(2,1)}, f32[8,256]{1,0:T(8,128)}, /*index=5*/bf16[4,304,128]{2,1,0:T(8,128)(2,1)}) custom-call(bf16[4,192,128]{2,1,0:T(8,128)(2,1)} %get-tuple-element.28.field_all, bf16[4,112,128]{2,1,0:T(8,128)(2,1)} %get-tuple-element.29.margin_all, ...), custom_call_target="tpu_custom_call" | custom-call | tf_op jit(solution)/shard_map/step/pallas_call | solution.py:349
  41.5 64.9 %reduce_all.1 = (bf16[9216,128]{1,0:T(8,128)(2,1)}, f32[8,256]{1,0:T(8,128)}, f32[192,128]{1,0:T(8,128)}, f32[96,128]{1,0:T(8,128)}) custom-call(bf16[9216,128]{1,0:T(8,128)(2,1)} %bitcast.5, f32[8,256]{1,0:T(8,128)} %get-tuple-element.33.bias, bf16[4,304,128]{2,1,0:T(8,128)(2,1)} %get-tuple-element.34.dpad, s32[64,128]{1,0:T(8,128)} %get-tuple-element.27.index), custom_call_target="tpu_custom_call" | custom-call | tf_op jit(solution)/shard_map/reduce_all/pallas_call | solution.py:614
  106.3 0.7 slice_reduce_fusion
  107.1 0.7 reshape_squeeze.3
  107.7 7.0 %finish.1 = (f32[9,256,512]{2,1,0:T(8,128)}, bf16[3,64,64]{2,1,0:T(8,128)(2,1)}, bf16[3,64,64]{2,1,0:T(8,128)(2,1)}) custom-call(bf16[9,4,256,128]{3,2,1,0:T(8,128)(2,1)} %bitcast.6, f32[192,128]{1,0:T(8,128)} %get-tuple-element.36.inner, f32[96,128]{1,0:T(8,128)} %get-tuple-element.37.sides), custom_call_target="tpu_custom_call" | custom-call | tf_op jit(solution)/shard_map/finish/pallas_call | solution.py:656

commit v2 on v1

v2 whole, which is shorter than its diff:
```python
import functools

import jax
import jax.numpy as jnp
from jax import lax
from jax.experimental import pallas as pl
from jax.experimental.pallas import tpu as pltpu
from jax.sharding import PartitionSpec as P

F32, BF16, I32 = jnp.float32, jnp.bfloat16, jnp.int32
MESH = pl.DeviceIdType.MESH
NY, NX, NZ = 2, 4, 8
NQ = NY * NX
NC = 4
TPD = 3
PIX = 64
RIM = 32 * TPD
MARGIN = 112
BODY = 80 * TPD
DROWS = BODY + 64
UNIT = 1024
JOBS = ("yxz", "xyz", "zxy", "yxz", "xyz", "zxy", "yxz", "xyz", "yxz")
VMEM_LIMIT = 56 * 1024 * 1024


def nn(a, b):
    return lax.dot_general(a, b, (((1,), (0,)), ((), ())), preferred_element_type=F32)


def tn(a, b):
    return lax.dot_general(a, b, (((0,), (0,)), ((), ())), preferred_element_type=F32)


def nt(a, b):
    return lax.dot_general(a, b, (((1,), (1,)), ((), ())), preferred_element_type=F32)


def iota(shape, dim):
    return lax.broadcasted_iota(I32, shape, dim)


def eye(n):
    return (iota((n, n), 0) == iota((n, n), 1)).astype(BF16)


def position():
    t = lax.axis_index("tile")
    z, q = lax.rem(t, NZ), lax.div(t, NZ)
    return q, lax.div(q, NX), lax.rem(q, NX), z, lax.axis_index("chan")


def peers():
    q, y, x, z, c = position()
    return {
        "z": lambda d: (q * NZ + lax.rem(z + d, NZ), c),
        "q": lambda d: (lax.rem(q + d, NQ) * NZ + z, c),
        "x": lambda d: ((y * NX + lax.rem(x + d, NX)) * NZ + z, c),
        "y": lambda d: ((lax.rem(y + d, NY) * NX + x) * NZ + z, c),
        "c": lambda d: (q * NZ + z, lax.rem(c + d, NC)),
    }


def greet(to):
    barrier = pltpu.get_barrier_semaphore()
    count = 0
    for axis, size in (("z", NZ), ("q", NQ), ("c", NC)):
        for d in range(1, size):
            pl.semaphore_signal(barrier, inc=1, device_id=to[axis](d), device_id_type=MESH)
            count += 1
    return count


def send(src, dst, send_sem, recv_sem, device):
    pltpu.make_async_remote_copy(
        src_ref=src,
        dst_ref=dst,
        send_sem=send_sem,
        recv_sem=recv_sem,
        device_id=device,
        device_id_type=MESH,
    ).start()


def await_bytes(like, sem):
    pltpu.make_async_copy(like, like, sem).wait()


def axis_size(axis):
    return {"x": NX, "y": NY, "z": NZ}[axis]


def rows_of(order, stage):
    rows = UNIT
    for axis in order[:stage]:
        rows //= axis_size(axis)
    return rows


def own_cells(inp, hid, cells, field, rim):
    ident = eye(PIX)
    for t in range(TPD):
        both = jnp.concatenate([inp[t], hid[t]], axis=0)
        cells[t * PIX : (t + 1) * PIX, :] = nt(ident, both)
    field[...] = cells[...].astype(BF16)
    for t in range(TPD):
        base = t * PIX
        sides = jnp.concatenate(
            [
                cells[base : base + 8, :],
                cells[pl.ds(base + 7, 8, stride=8), :],
                cells[base + 56 : base + 64, :],
                cells[pl.ds(base, 8, stride=8), :],
            ],
            axis=0,
        )
        rim[t * 32 : (t + 1) * 32, :] = sides.astype(BF16)


def source_cells(esrc, ecode, csrc, ccode, by_tile, index):
    lane, row = iota((4, 128), 1), iota((4, 128), 0)
    edge_lane = ((lane < 32) & (lax.div(lane, 8) == row)).astype(F32).astype(BF16)
    corner_lane = (lane - 32 == row).astype(F32).astype(BF16)

    def spread(edges, corners):
        wide = tn(edges[...].astype(F32).astype(BF16), edge_lane)
        wide += tn(corners[...].astype(F32).astype(BF16), corner_lane)
        return wide.astype(I32)

    source, code = spread(esrc, csrc), spread(ecode, ccode)
    lane = iota(source.shape, 1)
    cell = lane & 7
    along_side = (code >> 1) * 8 + jnp.where((code & 1) == 1, 7 - cell, cell)
    at_corner = jnp.where(
        code == 0, 0, jnp.where(code == 1, 7, jnp.where(code == 2, 23, 16))
    )
    by_tile[...] = source * 32 + jnp.where(lane < 32, along_side, at_corner)
    devices = index.shape[0]
    rows = [by_tile[pl.ds(i, devices, stride=TPD), :] for i in range(TPD)]
    index[...] = jnp.concatenate(
        [r[:, :32] for r in rows]
        + [r[:, 32:36] for r in rows]
        + [jnp.full((devices, 128 - 36 * TPD), -1000000, I32)],
        axis=1,
    )


def whole_kernel(
    inp,
    hid,
    cell_prev,
    kern_hbm,
    gate_bias,
    hidden_up,
    cell_up,
    esrc,
    ecode,
    csrc,
    ccode,
    hidden_out,
    cell_out,
    cell_grad_out,
    grad_out,
    bias_out,
    inner_out,
    side_out,
    kern,
    kern_sem,
    cells,
    field,
    rim,
    by_tile,
    index,
    table,
    picked,
    arrived,
    field_all,
    margin_all,
    wide,
    windows,
    accs,
    grad,
    bias,
    dpad,
    dpad_in,
    dsum,
    margin_own,
    margin_send,
    margin_in,
    slot_sum,
    slot_send,
    slot_in,
    bias_in_q,
    bias_mid,
    bias_in_z,
    *rest,
):
    jobs = len(JOBS)
    landing = [rest[5 * j : 5 * j + 3] for j in range(jobs)]
    passing = [rest[5 * j + 3 : 5 * j + 5] for j in range(jobs)]
    small_s, small_r, job_s, job_r = rest[5 * jobs :]
    q, y, x, z, c = position()
    here = {"x": x, "y": y, "z": z}
    to = peers()

    greeted = greet(to)
    load = pltpu.make_async_copy(kern_hbm, kern, kern_sem)
    load.start()
    own_cells(inp, hid, cells, field, rim)
    pl.semaphore_wait(pltpu.get_barrier_semaphore(), greeted)

    for d in range(1, NZ):
        send(rim, table.at[z], small_s.at[5], small_r.at[5], to["z"](d))
    for d in range(1, NC):
        send(field, field_all.at[c], small_s.at[6], small_r.at[6], to["c"](d))
    table[z] = rim[...]
    field_all[c] = field[...]
    source_cells(esrc, ecode, csrc, ccode, by_tile, index)

    first = q * (NZ * RIM)
    choosers = []
    for d in range(NQ):
        row = index[pl.ds(lax.rem(q + d, NQ) * NZ + z, 1), :]
        down = jnp.broadcast_to((row - first).astype(F32), (128, 128)).T
        choosers.append(
            jnp.concatenate(
                [
                    (down == (iota((128, 128), 1) + 128 * k).astype(F32)).astype(BF16)
                    for k in range(NZ * RIM // 128)
                ],
                axis=1,
            )
        )
    await_bytes(table.at[pl.ds(0, NZ - 1)], small_r.at[5])
    rims = table[...].reshape(NZ * RIM, 128)
    for d in list(range(1, NQ)) + [0]:
        picked[d] = nn(choosers[d], rims)[:MARGIN].astype(BF16)
        if d:
            send(picked.at[d], arrived.at[d - 1], small_s.at[7], small_r.at[7], to["q"](d))

    def lanes(ref, k):
        pair, half = 2 * (k % 2), 64 * (k // 2)
        return jnp.concatenate(
            [ref[pair][:, half : half + 64], ref[pair + 1][:, half : half + 64]], axis=1
        ).astype(F32)

    await_bytes(field_all.at[pl.ds(0, NC - 1)], small_r.at[6])
    for k in range(4):
        body = lanes(field_all, k)
        for t in range(TPD):
            wide[1, k, t * 80 + 8 : t * 80 + 72, :] = body[t * PIX : (t + 1) * PIX]

    await_bytes(arrived, small_r.at[7])
    total = picked[0].astype(F32)
    for d in range(1, NQ):
        total += arrived[d - 1].astype(F32)
    margin_all[c] = total.astype(BF16)
    for d in range(1, NC):
        send(margin_all.at[c], margin_all.at[c], small_s.at[8], small_r.at[8], to["c"](d))
    load.wait()
    await_bytes(margin_all.at[pl.ds(0, NC - 1)], small_r.at[8])

    for k in range(4):
        margin = lanes(margin_all, k)
        for t in range(TPD):
            base, at = t * 80, t * 32
            wide[1, k, base : base + 8, :] = margin[at : at + 8]
            wide[1, k, base + 72 : base + 80, :] = margin[at + 16 : at + 24]
        wide[0, k, 1:BODY, :] = wide[1, k, 0 : BODY - 1, :]
        wide[2, k, 0 : BODY - 1, :] = wide[1, k, 1:BODY, :]
        for t in range(TPD):
            base, at, corner = t * 80, t * 32, RIM + t * 4
            left, right = wide.at[0, k], wide.at[2, k]
            left[base : base + 1, :] = margin[corner : corner + 1]
            left[pl.ds(base + 8, 8, stride=8), :] = margin[at + 24 : at + 32]
            left[base + 72 : base + 73, :] = margin[corner + 3 : corner + 4]
            right[base + 7 : base + 8, :] = margin[corner + 1 : corner + 2]
            right[pl.ds(base + 15, 8, stride=8), :] = margin[at + 8 : at + 16]
            right[base + 79 : base + 80, :] = margin[corner + 2 : corner + 3]
    for o in range(9):
        a, b = o // 3, o % 3
        for k in range(4):
            for t in range(TPD):
                base = t * 80 + a * 8
                windows[o, t * PIX : (t + 1) * PIX, k * 128 : (k + 1) * 128] = wide[
                    b, k, base : base + PIX, :
                ].astype(BF16)

    def gate(k):
        column = jnp.broadcast_to(gate_bias[k : k + 1, :], (64, 64)).T
        return jnp.concatenate([column] * TPD, axis=1)

    gates = jnp.concatenate([gate(k) for k in range(4)], axis=0)
    for o in range(9):
        gates = gates + nt(kern[o], windows[o])
    in_gate = jax.nn.sigmoid(gates[0:64])
    forget = jax.nn.sigmoid(gates[64:128])
    cand = jnp.tanh(gates[128:192])
    out_gate = jax.nn.sigmoid(gates[192:256])
    before = jnp.concatenate([cell_prev[t] for t in range(TPD)], axis=1)
    above = jnp.concatenate([cell_up[t] for t in range(TPD)], axis=1)
    upstream = jnp.concatenate([hidden_up[t].astype(F32) for t in range(TPD)], axis=1)
    cell_new = forget * before + in_gate * cand
    squashed = jnp.tanh(cell_new)
    hidden_new = (out_gate * squashed).astype(BF16)
    dcell = above + upstream * out_gate * (1.0 - squashed * squashed)
    cell_grad = dcell * forget
    dgates = jnp.concatenate(
        [
            dcell * cand * in_gate * (1.0 - in_gate),
            dcell * before * forget * (1.0 - forget),
            dcell * in_gate * (1.0 - cand * cand),
            upstream * squashed * out_gate * (1.0 - out_gate),
        ],
        axis=0,
    ).astype(BF16)

    def start_of(j, stage):
        start, rows = j * UNIT, UNIT
        for axis in JOBS[j][:stage]:
            rows //= axis_size(axis)
            start = start + here[axis] * rows
        return pl.multiple_of(start, 16) if stage else start

    def scatter(j, stage):
        axis = JOBS[j][stage]
        size, rows = axis_size(axis), rows_of(JOBS[j], stage + 1)
        for d in range(1, size):
            chunk = lax.rem(here[axis] + d, size) * rows
            if stage == 0:
                src = grad.at[pl.ds(pl.multiple_of(j * UNIT + chunk, 16), rows)]
            else:
                src = passing[j][stage - 1].at[pl.ds(pl.multiple_of(chunk, 16), rows)]
            send(
                src,
                landing[j][stage].at[d - 1],
                job_s.at[j, stage],
                job_r.at[j, stage],
                to[axis](d),
            )

    def gather(j, stage):
        axis = JOBS[j][stage]
        size, rows = axis_size(axis), rows_of(JOBS[j], stage + 1)
        mine = grad_out.at[pl.ds(start_of(j, stage + 1), rows)]
        for d in range(1, size):
            send(mine, mine, job_s.at[j, 3 + stage], job_r.at[j, 3 + stage], to[axis](d))

    def add_up(j, stage):
        axis = JOBS[j][stage]
        rows = rows_of(JOBS[j], stage + 1)
        await_bytes(landing[j][stage], job_r.at[j, stage])
        mine = here[axis] * rows
        if stage == 0:
            source, mine = grad, j * UNIT + mine
        else:
            source = passing[j][stage - 1]
        total = source[pl.ds(pl.multiple_of(mine, 16), rows), :].astype(F32)
        for d in range(axis_size(axis) - 1):
            total += landing[j][stage][d].astype(F32)
        if stage < 2:
            passing[j][stage][...] = total.astype(BF16)
        else:
            grad_out[pl.ds(start_of(j, 3), rows), :] = total.astype(BF16)

    def gathered(j, stage):
        axis = JOBS[j][stage]
        rows = rows_of(JOBS[j], stage + 1) * (axis_size(axis) - 1)
        await_bytes(grad_out.at[pl.ds(0, rows)], job_r.at[j, 3 + stage])

    for j in range(jobs):
        product = nn(dgates, windows[j]).astype(BF16)
        for k in range(4):
            at = j * UNIT + k * 256
            grad[at : at + 256, :] = product[:, k * 128 : (k + 1) * 128]
        scatter(j, 0)

    turned = nt(eye(TPD * PIX), dgates).astype(BF16)
    accs[...] = jnp.zeros(accs.shape, F32)
    for o in range(9):
        a, b = o // 3, o % 3
        product = nn(turned, kern[o])
        for k in range(4):
            for t in range(TPD):
                base = 8 + t * 80 + a * 8
                accs[b, k, base : base + PIX, :] += product[
                    t * PIX : (t + 1) * PIX, k * 128 : (k + 1) * 128
                ]
    column = iota((BODY, 128), 0) & 7
    blocks = []
    for k in range(4):
        body = accs[1, k, 8 : 8 + BODY, :]
        body += jnp.where(column < 7, accs[0, k, 9 : 9 + BODY, :], 0.0)
        body += jnp.where(column > 0, accs[2, k, 7 : 7 + BODY, :], 0.0)
        left, right = accs.at[0, k], accs.at[2, k]
        blocks.append(
            (
                body,
                left[pl.ds(8, 32, stride=8), :],
                right[pl.ds(15, 32, stride=8), :],
            )
        )
    for e in range(NC):
        half = slice((e % 2) * 64, (e % 2) * 64 + 64)
        start = 0
        for one, two in zip(blocks[e // 2], blocks[2 + e // 2]):
            rows = one.shape[0]
            dpad[e, start : start + rows, :] = jnp.concatenate(
                [one[:, half], two[:, half]], axis=1
            ).astype(BF16)
            start += rows
    for d in range(1, NC):
        send(
            dpad.at[lax.rem(c + d, NC)],
            dpad_in.at[d - 1],
            small_s.at[0],
            small_r.at[0],
            to["c"](d),
        )
    bias[...] = nt(jnp.ones((8, TPD * PIX), BF16), dgates)
    for d in range(1, NQ):
        send(bias, bias_in_q.at[d - 1], small_s.at[1], small_r.at[1], to["q"](d))
    for t in range(TPD):
        at = slice(t * PIX, (t + 1) * PIX)
        hidden_out[t] = hidden_new[:, at]
        cell_out[t] = cell_new[:, at]
        cell_grad_out[t] = cell_grad[:, at]

    await_bytes(dpad_in, small_r.at[0])
    total = dpad[c].astype(F32)
    for d in range(NC - 1):
        total += dpad_in[d].astype(F32)
    dsum[...] = total
    left, right = BODY, BODY + 32
    margin_own[...] = jnp.zeros(margin_own.shape, F32)
    for t in range(TPD):
        base, at, corner, col = t * 80, t * 32, RIM + t * 4, t * 10
        margin_own[at : at + 8, :] = dsum[base : base + 8, :]
        margin_own[at + 8 : at + 16, :] = dsum[right + col + 1 : right + col + 9, :]
        margin_own[at + 16 : at + 24, :] = dsum[base + 72 : base + 80, :]
        margin_own[at + 24 : at + 32, :] = dsum[left + col + 1 : left + col + 9, :]
        margin_own[corner : corner + 1, :] = dsum[left + col : left + col + 1, :]
        margin_own[corner + 1 : corner + 2, :] = dsum[right + col : right + col + 1, :]
        margin_own[corner + 2 : corner + 3, :] = dsum[right + col + 9 : right + col + 10, :]
        margin_own[corner + 3 : corner + 4, :] = dsum[left + col + 9 : left + col + 10, :]
        inner_out[t * PIX : (t + 1) * PIX, :] = dsum[base + 8 : base + 72, :]
    margin_send[...] = margin_own[...].astype(BF16)
    for d in range(1, NQ):
        send(margin_send, margin_in.at[d - 1], small_s.at[2], small_r.at[2], to["q"](d))

    for j in range(jobs):
        add_up(j, 0)
        scatter(j, 1)

    choosers = []
    for d in range(NQ):
        row = index[pl.ds(lax.rem(q + NQ - d, NQ) * NZ + z, 1), :][:, :MARGIN]
        chooser = (iota((NZ * RIM, MARGIN), 0) == row - first).astype(F32).astype(BF16)
        choosers.append(chooser)
    await_bytes(margin_in, small_r.at[2])
    sums = nn(choosers[0], margin_send[...])
    for d in range(1, NQ):
        sums += nn(choosers[d], margin_in[d - 1])
    slot_sum[...] = sums.reshape(NZ, RIM, 128)
    slot_send[...] = slot_sum[...].astype(BF16)
    for d in range(1, NZ):
        send(
            slot_send.at[lax.rem(z + d, NZ)],
            slot_in.at[d - 1],
            small_s.at[3],
            small_r.at[3],
            to["z"](d),
        )
    await_bytes(bias_in_q, small_r.at[1])
    total = bias[...]
    for d in range(NQ - 1):
        total += bias_in_q[d]
    bias_mid[...] = total
    for d in range(1, NZ):
        send(bias_mid, bias_in_z.at[d - 1], small_s.at[4], small_r.at[4], to["z"](d))

    for j in range(jobs):
        add_up(j, 1)
        scatter(j, 2)

    await_bytes(slot_in, small_r.at[3])
    total = slot_sum[z]
    for d in range(NZ - 1):
        total += slot_in[d].astype(F32)
    side_out[...] = total
    await_bytes(bias_in_z, small_r.at[4])
    total = bias_mid[...]
    for d in range(NZ - 1):
        total += bias_in_z[d]
    bias_out[...] = total

    for j in range(jobs):
        add_up(j, 2)
        gather(j, 2)
    for stage in (2, 1):
        for j in range(jobs):
            gathered(j, stage)
            gather(j, stage - 1)
    for j in range(jobs):
        gathered(j, 0)

    await_bytes(dpad_in, small_s.at[0])
    await_bytes(bias_in_q, small_s.at[1])
    await_bytes(margin_in, small_s.at[2])
    await_bytes(slot_in, small_s.at[3])
    await_bytes(bias_in_z, small_s.at[4])
    await_bytes(table.at[pl.ds(0, NZ - 1)], small_s.at[5])
    await_bytes(field_all.at[pl.ds(0, NC - 1)], small_s.at[6])
    await_bytes(arrived, small_s.at[7])
    await_bytes(margin_all.at[pl.ds(0, NC - 1)], small_s.at[8])
    for j in range(jobs):
        for stage in range(3):
            await_bytes(landing[j][stage], job_s.at[j, stage])
            axis = JOBS[j][stage]
            rows = rows_of(JOBS[j], stage + 1) * (axis_size(axis) - 1)
            await_bytes(grad_out.at[pl.ds(0, rows)], job_s.at[j, 3 + stage])


def whole(inp, hid, cell_prev, kern, gate_bias, hidden_up, cell_up, lists):
    vmem = pl.BlockSpec(memory_space=pltpu.VMEM)
    state = cell_prev.shape
    devices = NQ * NZ
    scratch = [
        pltpu.VMEM(kern.shape, BF16),
        pltpu.SemaphoreType.DMA,
        pltpu.VMEM((TPD * PIX, 128), F32),
        pltpu.VMEM((TPD * PIX, 128), BF16),
        pltpu.VMEM((RIM, 128), BF16),
        pltpu.VMEM((devices * TPD, 128), I32),
        pltpu.VMEM((devices, 128), I32),
        pltpu.VMEM((NZ, RIM, 128), BF16),
        pltpu.VMEM((NQ, MARGIN, 128), BF16),
        pltpu.VMEM((NQ - 1, MARGIN, 128), BF16),
        pltpu.VMEM((NC, TPD * PIX, 128), BF16),
        pltpu.VMEM((NC, MARGIN, 128), BF16),
        pltpu.VMEM((3, 4, BODY, 128), F32),
        pltpu.VMEM((9, TPD * PIX, 512), BF16),
        pltpu.VMEM((3, 4, 8 + BODY + 32, 128), F32),
        pltpu.VMEM((9 * UNIT, 128), BF16),
        pltpu.VMEM((8, 256), F32),
        pltpu.VMEM((NC, DROWS, 128), BF16),
        pltpu.VMEM((NC - 1, DROWS, 128), BF16),
        pltpu.VMEM((DROWS, 128), F32),
        pltpu.VMEM((MARGIN, 128), F32),
        pltpu.VMEM((MARGIN, 128), BF16),
        pltpu.VMEM((NQ - 1, MARGIN, 128), BF16),
        pltpu.VMEM((NZ, RIM, 128), F32),
        pltpu.VMEM((NZ, RIM, 128), BF16),
        pltpu.VMEM((NZ - 1, RIM, 128), BF16),
        pltpu.VMEM((NQ - 1, 8, 256), F32),
        pltpu.VMEM((8, 256), F32),
        pltpu.VMEM((NZ - 1, 8, 256), F32),
    ]
    for order in JOBS:
        for stage in range(3):
            rows = rows_of(order, stage + 1)
            scratch.append(pltpu.VMEM((axis_size(order[stage]) - 1, rows, 128), BF16))
        for stage in range(2):
            scratch.append(pltpu.VMEM((rows_of(order, stage + 1), 128), BF16))
    scratch += [
        pltpu.SemaphoreType.DMA((9,)),
        pltpu.SemaphoreType.DMA((9,)),
        pltpu.SemaphoreType.DMA((len(JOBS), 6)),
        pltpu.SemaphoreType.DMA((len(JOBS), 6)),
    ]
    return pl.pallas_call(
        whole_kernel,
        out_shape=(
            jax.ShapeDtypeStruct(state, BF16),
            jax.ShapeDtypeStruct(state, F32),
            jax.ShapeDtypeStruct(state, F32),
            jax.ShapeDtypeStruct((9 * UNIT, 128), BF16),
            jax.ShapeDtypeStruct((8, 256), F32),
            jax.ShapeDtypeStruct((TPD * PIX, 128), F32),
            jax.ShapeDtypeStruct((RIM, 128), F32),
        ),
        in_specs=[vmem] * 3 + [pl.BlockSpec(memory_space=pl.ANY)] + [vmem] * 7,
        out_specs=(vmem,) * 7,
        scratch_shapes=scratch,
        compiler_params=pltpu.CompilerParams(
            collective_id=0, has_side_effects=True, vmem_limit_bytes=VMEM_LIMIT
        ),
        name="whole",
    )(inp, hid, cell_prev, kern, gate_bias, hidden_up, cell_up, *lists)


def finish_kernel(
    hidden,
    cell,
    cell_grad,
    grad,
    bias,
    inner,
    sides,
    hidden_out,
    cell_out,
    cell_grad_out,
    grad_out,
    bias_out,
    input_out,
    prior_out,
    held,
    wide,
    cells,
    sems_in,
    sems_out,
):
    def fetch(o):
        return pltpu.make_async_copy(grad.at[o], held.at[o], sems_in.at[o])

    def put(o):
        return pltpu.make_async_copy(wide.at[o], grad_out.at[o], sems_out.at[o])

    for o in range(9):
        fetch(o).start()
    for o in range(9):
        fetch(o).wait()
        for k in range(4):
            wide[o, :, k * 128 : (k + 1) * 128] = held[o, k].astype(F32)
        put(o).start()
    hidden_out[...] = hidden[...]
    cell_out[...] = cell[...]
    cell_grad_out[...] = cell_grad[...]
    for k in range(4):
        bias_out[k : k + 1, :] = bias[0:1, k * 64 : (k + 1) * 64]
    cells[...] = inner[...]
    for t in range(TPD):
        base, at = t * PIX, t * 32
        cells[base : base + 8, :] += sides[at : at + 8, :]
        cells[pl.ds(base + 7, 8, stride=8), :] += sides[at + 8 : at + 16, :]
        cells[base + 56 : base + 64, :] += sides[at + 16 : at + 24, :]
        cells[pl.ds(base, 8, stride=8), :] += sides[at + 24 : at + 32, :]
    ident = eye(128)
    for t in range(TPD):
        rounded = cells[t * PIX : (t + 1) * PIX, :].astype(BF16)
        turned = nt(ident, rounded).astype(BF16)
        input_out[t] = turned[0:64]
        prior_out[t] = turned[64:128]
    for o in range(9):
        put(o).wait()


def finish(hidden, cell, cell_grad, grad, bias, inner, sides):
    vmem, hbm = pl.BlockSpec(memory_space=pltpu.VMEM), pl.BlockSpec(memory_space=pl.ANY)
    return pl.pallas_call(
        finish_kernel,
        out_shape=(
            jax.ShapeDtypeStruct(hidden.shape, BF16),
            jax.ShapeDtypeStruct(hidden.shape, F32),
            jax.ShapeDtypeStruct(hidden.shape, F32),
            jax.ShapeDtypeStruct((9, 256, 512), F32),
            jax.ShapeDtypeStruct((4, 64), F32),
            jax.ShapeDtypeStruct(hidden.shape, BF16),
            jax.ShapeDtypeStruct(hidden.shape, BF16),
        ),
        in_specs=[vmem] * 3 + [hbm] + [vmem] * 3,
        out_specs=(vmem,) * 3 + (hbm,) + (vmem,) * 3,
        scratch_shapes=[
            pltpu.VMEM(grad.shape, BF16),
            pltpu.VMEM((9, 256, 512), F32),
            pltpu.VMEM(inner.shape, F32),
            pltpu.SemaphoreType.DMA((9,)),
            pltpu.SemaphoreType.DMA((9,)),
        ],
        compiler_params=pltpu.CompilerParams(vmem_limit_bytes=VMEM_LIMIT),
        name="finish",
    )(hidden, cell, cell_grad, grad, bias, inner, sides)


def local(
    inputs,
    prior_hidden_state,
    cell_prev,
    kernel,
    gate_bias,
    hidden_upstream,
    cell_upstream,
    edge_source,
    edge_code,
    corner_source,
    corner_code,
):
    hidden_new, cell_new, cell_grad, grad, bias, inner, sides = whole(
        inputs,
        prior_hidden_state,
        cell_prev,
        kernel.reshape(9, 256, 512),
        gate_bias,
        hidden_upstream,
        cell_upstream,
        [a.T for a in (edge_source, edge_code, corner_source, corner_code)],
    )
    hidden_new, cell_new, cell_grad, kernel_grad, bias_grad, input_grad, hidden_grad = finish(
        hidden_new, cell_new, cell_grad, grad.reshape(9, 4, 256, 128), bias, inner, sides
    )
    return (
        hidden_new,
        cell_new,
        kernel_grad.reshape(9, 4, 64, 512),
        bias_grad,
        input_grad,
        hidden_grad,
        cell_grad,
    )


def solution(mesh):
    tiles, whole = P("tile", "chan", None), P()
    gates = P(None, None, "chan", None)
    bias = P(None, "chan")
    in_specs = (tiles, tiles, tiles, gates, bias, tiles, tiles, whole, whole, whole, whole)
    out_specs = (tiles, tiles, gates, bias, tiles, tiles, tiles)
    return jax.shard_map(local, mesh=mesh, in_specs=in_specs, out_specs=out_specs, check_vma=False)
```

time: 115 us -> 92.5 us (0.80)
  Pallas kernels: 105 us -> 91.3 us
  local copies, waits for them, and re-layouts: 8.63 us -> 0 us
    pallas_call x5 -> x2, Pallas kernels: 105 us -> 91.3 us  [the longest x1 86.2 us: whole(): pl.pallas_call(whole_kernel, out_shape=(jax.ShapeDtypeStruct(state, BF16)...]
    unnamed x4 -> x0, local copies, waits for them, and re-layouts: 5.78 us -> none
    reshape x1 -> x0, local copies, waits for them, and re-layouts: 1.47 us -> none  [local(): gate_bias.reshape(256, 1)]
where the time goes in v2:
time: 92.5 us; the launch traced here: 92 us
  Pallas kernels  91.3 us (99%)
    pallas_call x1, Pallas kernels, whole(): pl.pallas_call(whole_kernel, out_shape=(jax.ShapeDtypeStruct(state, BF16)...  86.2 us
    pallas_call x1, Pallas kernels, finish(): pl.pallas_call(finish_kernel, out_shape=(jax.ShapeDtypeStruct(hidden.shap...  5.1 us

profile of v2, /device:TPU:32, one launch (start us, length us, event | category | flops | bytes accessed | tf_op | source)
XLA Modules:
  0.0 92.0 jit_solution(15822565203818960657)
XLA Ops:
  0.6 86.2 %whole.1 = (bf16[3,64,64]{2,1,0:T(8,128)(2,1)}, f32[3,64,64]{2,1,0:T(8,128)}, f32[3,64,64]{2,1,0:T(8,128)}, bf16[9216,128]{1,0:T(8,128)(2,1)}, f32[8,256]{1,0:T(...) custom-call(bf16[3,64,64]{2,1,0:T(8,128)(2,1)} %inp.1, bf16[3,64,64]{2,1,0:T(8,128)(2,1)} %hid.1, f32[3,64,64]{2,1,0:T(8,128)} %cell_prev.1, ...), custom_call_target="tpu_custom_call" | custom-call | tf_op jit(solution)/shard_map/whole/pallas_call | solution.py:570
  86.9 5.1 %finish.1 = (bf16[3,64,64]{2,1,0:T(8,128)(2,1)}, f32[3,64,64]{2,1,0:T(8,128)}, f32[3,64,64]{2,1,0:T(8,128)}, f32[9,256,512]{2,1,0:T(8,128)}, f32[4,64]{1,0:T(4,1...) custom-call(bf16[3,64,64]{2,1,0:T(8,128)(2,1)} %get-tuple-element.21.hidden, ...), custom_call_target="tpu_custom_call" | custom-call | tf_op jit(solution)/shard_map/finish/pallas_call | solution.py:649

commit v3 on v2

--- a/solution.py
+++ b/solution.py
@@ -18,8 +18,9 @@
 MARGIN = 112
 BODY = 80 * TPD
 DROWS = BODY + 64
-UNIT = 1024
-JOBS = ("yxz", "xyz", "zxy", "yxz", "xyz", "zxy", "yxz", "xyz", "yxz")
+SHARE = 16
+GROUPS = ((0, 3), (3, 6), (6, 9))
+ORDERS = ("yxz", "zyx", "yxz", "zxy", "yxz", "zyx", "yxz", "zxy", "zyx")
 VMEM_LIMIT = 56 * 1024 * 1024
 
 
@@ -89,11 +90,8 @@
     return {"x": NX, "y": NY, "z": NZ}[axis]
 
 
-def rows_of(order, stage):
-    rows = UNIT
-    for axis in order[:stage]:
-        rows //= axis_size(axis)
-    return rows
+def ring_steps(o):
+    return (NZ // 2, NZ // 2 - 1) if o % 2 == 0 else (NZ // 2 - 1, NZ // 2)
 
 
 def own_cells(inp, hid, cells, field, rim):
@@ -178,7 +176,15 @@
     wide,
     windows,
     accs,
+    field_near,
+    margin_near,
+    wide_near,
+    windows_near,
+    turned_own,
+    turned_near,
     grad,
+    grad_in,
+    gauge,
     bias,
     dpad,
     dpad_in,
@@ -192,15 +198,20 @@
     bias_in_q,
     bias_mid,
     bias_in_z,
-    *rest,
+    small_s,
+    small_r,
+    sum_s,
+    sum_r,
+    all_s,
+    all_r,
+    ring_s,
+    ring_r,
 ):
-    jobs = len(JOBS)
-    landing = [rest[5 * j : 5 * j + 3] for j in range(jobs)]
-    passing = [rest[5 * j + 3 : 5 * j + 5] for j in range(jobs)]
-    small_s, small_r, job_s, job_r = rest[5 * jobs :]
     q, y, x, z, c = position()
-    here = {"x": x, "y": y, "z": z}
     to = peers()
+
+    def quarter(d):
+        return lax.rem(lax.rem(q + d, NQ), NX)
 
     greeted = greet(to)
     load = pltpu.make_async_copy(kern_hbm, kern, kern_sem)
@@ -244,6 +255,15 @@
         ).astype(F32)
 
     await_bytes(field_all.at[pl.ds(0, NC - 1)], small_r.at[6])
+    for d in range(1, NQ):
+        send(
+            field_all.at[quarter(d)],
+            field_near.at[d],
+            small_s.at[9],
+            small_r.at[9],
+            to["q"](d),
+        )
+    field_near[0] = field_all[x]
     for k in range(4):
         body = lanes(field_all, k)
         for t in range(TPD):
@@ -258,6 +278,15 @@
         send(margin_all.at[c], margin_all.at[c], small_s.at[8], small_r.at[8], to["c"](d))
     load.wait()
     await_bytes(margin_all.at[pl.ds(0, NC - 1)], small_r.at[8])
+    for d in range(1, NQ):
+        send(
+            margin_all.at[quarter(d)],
+            margin_near.at[d],
+            small_s.at[10],
+            small_r.at[10],
+            to["q"](d),
+        )
+    margin_near[0] = margin_all[x]
 
     for k in range(4):
         margin = lanes(margin_all, k)
@@ -314,67 +343,19 @@
         axis=0,
     ).astype(BF16)
 
-    def start_of(j, stage):
-        start, rows = j * UNIT, UNIT
-        for axis in JOBS[j][:stage]:
-            rows //= axis_size(axis)
-            start = start + here[axis] * rows
-        return pl.multiple_of(start, 16) if stage else start
-
-    def scatter(j, stage):
-        axis = JOBS[j][stage]
-        size, rows = axis_size(axis), rows_of(JOBS[j], stage + 1)
-        for d in range(1, size):
-            chunk = lax.rem(here[axis] + d, size) * rows
-            if stage == 0:
-                src = grad.at[pl.ds(pl.multiple_of(j * UNIT + chunk, 16), rows)]
-            else:
-                src = passing[j][stage - 1].at[pl.ds(pl.multiple_of(chunk, 16), rows)]
-            send(
-                src,
-                landing[j][stage].at[d - 1],
-                job_s.at[j, stage],
-                job_r.at[j, stage],
-                to[axis](d),
-            )
-
-    def gather(j, stage):
-        axis = JOBS[j][stage]
-        size, rows = axis_size(axis), rows_of(JOBS[j], stage + 1)
-        mine = grad_out.at[pl.ds(start_of(j, stage + 1), rows)]
-        for d in range(1, size):
-            send(mine, mine, job_s.at[j, 3 + stage], job_r.at[j, 3 + stage], to[axis](d))
-
-    def add_up(j, stage):
-        axis = JOBS[j][stage]
-        rows = rows_of(JOBS[j], stage + 1)
-        await_bytes(landing[j][stage], job_r.at[j, stage])
-        mine = here[axis] * rows
-        if stage == 0:
-            source, mine = grad, j * UNIT + mine
-        else:
-            source = passing[j][stage - 1]
-        total = source[pl.ds(pl.multiple_of(mine, 16), rows), :].astype(F32)
-        for d in range(axis_size(axis) - 1):
-            total += landing[j][stage][d].astype(F32)
-        if stage < 2:
-            passing[j][stage][...] = total.astype(BF16)
-        else:
-            grad_out[pl.ds(start_of(j, 3), rows), :] = total.astype(BF16)
-
-    def gathered(j, stage):
-        axis = JOBS[j][stage]
-        rows = rows_of(JOBS[j], stage + 1) * (axis_size(axis) - 1)
-        await_bytes(grad_out.at[pl.ds(0, rows)], job_r.at[j, 3 + stage])
-
-    for j in range(jobs):
-        product = nn(dgates, windows[j]).astype(BF16)
-        for k in range(4):
-            at = j * UNIT + k * 256
-            grad[at : at + 256, :] = product[:, k * 128 : (k + 1) * 128]
-        scatter(j, 0)
-
     turned = nt(eye(TPD * PIX), dgates).astype(BF16)
+    for h in range(NY):
+        turned_own[h] = turned[:, h * 128 : (h + 1) * 128]
+    for d in range(1, NQ):
+        send(
+            turned_own.at[lax.div(lax.rem(q + d, NQ), NX)],
+            turned_near.at[d],
+            small_s.at[11],
+            small_r.at[11],
+            to["q"](d),
+        )
+    turned_near[0] = turned_own[y]
+
     accs[...] = jnp.zeros(accs.shape, F32)
     for o in range(9):
         a, b = o // 3, o % 3
@@ -425,6 +406,53 @@
         cell_out[t] = cell_new[:, at]
         cell_grad_out[t] = cell_grad[:, at]
 
+    await_bytes(field_near.at[pl.ds(0, NQ - 1)], small_r.at[9])
+    await_bytes(margin_near.at[pl.ds(0, NQ - 1)], small_r.at[10])
+
+    def windows_of(s, carry):
+        body, margin = field_near[s].astype(F32), margin_near[s].astype(F32)
+        left, right = wide_near.at[0], wide_near.at[2]
+        for t in range(TPD):
+            base, at = t * 80, t * 32
+            wide_near[1, base : base + 8, :] = margin[at : at + 8]
+            wide_near[1, base + 8 : base + 72, :] = body[t * PIX : (t + 1) * PIX]
+            wide_near[1, base + 72 : base + 80, :] = margin[at + 16 : at + 24]
+        wide_near[0, 1:BODY, :] = wide_near[1, 0 : BODY - 1, :]
+        wide_near[2, 0 : BODY - 1, :] = wide_near[1, 1:BODY, :]
+        for t in range(TPD):
+            base, at, corner = t * 80, t * 32, RIM + t * 4
+            left[base : base + 1, :] = margin[corner : corner + 1]
+            left[pl.ds(base + 8, 8, stride=8), :] = margin[at + 24 : at + 32]
+            left[base + 72 : base + 73, :] = margin[corner + 3 : corner + 4]
+            right[base + 7 : base + 8, :] = margin[corner + 1 : corner + 2]
+            right[pl.ds(base + 15, 8, stride=8), :] = margin[at + 8 : at + 16]
+            right[base + 79 : base + 80, :] = margin[corner + 2 : corner + 3]
+        for o in range(9):
+            for t in range(TPD):
+                base = t * 80 + (o // 3) * 8
+                row = pl.multiple_of(s * (TPD * PIX) + t * PIX, PIX)
+                windows_near[pl.ds(row, PIX), o * 128 : (o + 1) * 128] = wide_near[
+                    o % 3, base : base + PIX, :
+                ].astype(BF16)
+        return carry
+
+    lax.fori_loop(0, NQ, windows_of, 0)
+    await_bytes(turned_near.at[pl.ds(0, NQ - 1)], small_r.at[11])
+    near = nt(eye(128), turned_near[...].reshape(NQ * TPD * PIX, 128)).astype(BF16)
+    for g, (low, high) in enumerate(GROUPS):
+        product = nn(near, windows_near[:, low * 128 : high * 128]).astype(BF16)
+        for o in range(low, high):
+            grad[o] = product[:, (o - low) * 128 : (o - low + 1) * 128]
+        for d in range(1, NZ):
+            at = pl.multiple_of(lax.rem(z + d, NZ) * SHARE, SHARE)
+            send(
+                grad.at[pl.ds(low, high - low), pl.ds(at, SHARE)],
+                grad_in.at[d - 1, pl.ds(low, high - low)],
+                sum_s.at[g],
+                sum_r.at[g],
+                to["z"](d),
+            )
+
     await_bytes(dpad_in, small_r.at[0])
     total = dpad[c].astype(F32)
     for d in range(NC - 1):
@@ -446,10 +474,6 @@
     margin_send[...] = margin_own[...].astype(BF16)
     for d in range(1, NQ):
         send(margin_send, margin_in.at[d - 1], small_s.at[2], small_r.at[2], to["q"](d))
-
-    for j in range(jobs):
-        add_up(j, 0)
-        scatter(j, 1)
 
     choosers = []
     for d in range(NQ):
@@ -478,9 +502,61 @@
     for d in range(1, NZ):
         send(bias_mid, bias_in_z.at[d - 1], small_s.at[4], small_r.at[4], to["z"](d))
 
-    for j in range(jobs):
-        add_up(j, 1)
-        scatter(j, 2)
+    def box(o, full, at_z=None):
+        return grad_out.at[
+            o,
+            slice(None) if "x" in full else x,
+            slice(None) if "y" in full else y,
+            slice(None) if "z" in full else (z if at_z is None else at_z),
+        ]
+
+    def box_rows(full):
+        rows = SHARE
+        for axis in full:
+            rows *= axis_size(axis)
+        return rows
+
+    def bytes_of(rows):
+        return gauge.at[pl.ds(0, rows)]
+
+    def on_ring(o, stage):
+        return stage == 2 and ORDERS[o][2] == "z"
+
+    def ring_send(o, step, side):
+        share = lax.rem(z + NZ + (1 - step if side == 0 else step - 1), NZ)
+        mine = box(o, "xy", share)
+        at = (o, side * (NZ // 2) + step - 1)
+        send(mine, mine, ring_s.at[at], ring_r.at[at], to["z"](1 if side == 0 else NZ - 1))
+
+    def ring_wait(o, step, side):
+        await_bytes(bytes_of(box_rows("xy")), ring_r.at[o, side * (NZ // 2) + step - 1])
+
+    def gather(o, stage):
+        if on_ring(o, stage):
+            for side in range(2):
+                ring_send(o, 1, side)
+            return
+        axis, full = ORDERS[o][stage], ORDERS[o][:stage]
+        mine = box(o, full)
+        for d in range(1, axis_size(axis)):
+            send(mine, mine, all_s.at[o, stage], all_r.at[o, stage], to[axis](d))
+
+    def stage_bytes(o, stage):
+        axis, full = ORDERS[o][stage], ORDERS[o][:stage]
+        return bytes_of(box_rows(full) * (axis_size(axis) - 1))
+
+    def gathered(o, stage):
+        await_bytes(stage_bytes(o, stage), all_r.at[o, stage])
+
+    for g, (low, high) in enumerate(GROUPS):
+        some = pl.ds(low, high - low)
+        await_bytes(grad_in.at[:, some], sum_r.at[g])
+        total = grad[some, pl.ds(pl.multiple_of(z * SHARE, SHARE), SHARE), :].astype(F32)
+        for d in range(NZ - 1):
+            total += grad_in[d, some].astype(F32)
+        for o in range(low, high):
+            grad_out[o, x, y, z] = total[o - low].astype(BF16)
+            gather(o, 0)
 
     await_bytes(slot_in, small_r.at[3])
     total = slot_sum[z]
@@ -493,15 +569,21 @@
         total += bias_in_z[d]
     bias_out[...] = total
 
-    for j in range(jobs):
-        add_up(j, 2)
-        gather(j, 2)
-    for stage in (2, 1):
-        for j in range(jobs):
-            gathered(j, stage)
-            gather(j, stage - 1)
-    for j in range(jobs):
-        gathered(j, 0)
+    for stage in (0, 1):
+        for o in range(9):
+            gathered(o, stage)
+            gather(o, stage + 1)
+    for step in range(1, NZ // 2 + 1):
+        for o in range(9):
+            if on_ring(o, 2):
+                for side in range(2):
+                    if step <= ring_steps(o)[side]:
+                        ring_wait(o, step, side)
+                    if step < ring_steps(o)[side]:
+                        ring_send(o, step + 1, side)
+    for o in range(9):
+        if not on_ring(o, 2):
+            gathered(o, 2)
 
     await_bytes(dpad_in, small_s.at[0])
     await_bytes(bias_in_q, small_s.at[1])
@@ -512,12 +594,20 @@
     await_bytes(field_all.at[pl.ds(0, NC - 1)], small_s.at[6])
     await_bytes(arrived, small_s.at[7])
     await_bytes(margin_all.at[pl.ds(0, NC - 1)], small_s.at[8])
-    for j in range(jobs):
+    for near, sem in ((field_near, 9), (margin_near, 10), (turned_near, 11)):
+        await_bytes(near.at[pl.ds(0, NQ - 1)], small_s.at[sem])
+    for g, (low, high) in enumerate(GROUPS):
+        await_bytes(grad_in.at[:, pl.ds(low, high - low)], sum_s.at[g])
+    for o in range(9):
         for stage in range(3):
-            await_bytes(landing[j][stage], job_s.at[j, stage])
-            axis = JOBS[j][stage]
-            rows = rows_of(JOBS[j], stage + 1) * (axis_size(axis) - 1)
-            await_bytes(grad_out.at[pl.ds(0, rows)], job_s.at[j, 3 + stage])
+            if not on_ring(o, stage):
+                await_bytes(stage_bytes(o, stage), all_s.at[o, stage])
+                continue
+            for side in range(2):
+                for step in range(ring_steps(o)[side]):
+                    await_bytes(
+                        bytes_of(box_rows("xy")), ring_s.at[o, side * (NZ // 2) + step]
+                    )
 
 
 def whole(inp, hid, cell_prev, kern, gate_bias, hidden_up, cell_up, lists):
@@ -540,7 +630,15 @@
         pltpu.VMEM((3, 4, BODY, 128), F32),
         pltpu.VMEM((9, TPD * PIX, 512), BF16),
         pltpu.VMEM((3, 4, 8 + BODY + 32, 128), F32),
-        pltpu.VMEM((9 * UNIT, 128), BF16),
+        pltpu.VMEM((NQ, TPD * PIX, 128), BF16),
+        pltpu.VMEM((NQ, MARGIN, 128), BF16),
+        pltpu.VMEM((3, BODY, 128), F32),
+        pltpu.VMEM((NQ * TPD * PIX, 9 * 128), BF16),
+        pltpu.VMEM((NY, TPD * PIX, 128), BF16),
+        pltpu.VMEM((NQ, TPD * PIX, 128), BF16),
+        pltpu.VMEM((9, 128, 128), BF16),
+        pltpu.VMEM((NZ - 1, 9, SHARE, 128), BF16),
+        pltpu.VMEM((1024, 128), BF16),
         pltpu.VMEM((8, 256), F32),
         pltpu.VMEM((NC, DROWS, 128), BF16),
         pltpu.VMEM((NC - 1, DROWS, 128), BF16),
@@ -555,25 +653,15 @@
         pltpu.VMEM((8, 256), F32),
         pltpu.VMEM((NZ - 1, 8, 256), F32),
     ]
-    for order in JOBS:
-        for stage in range(3):
-            rows = rows_of(order, stage + 1)
-            scratch.append(pltpu.VMEM((axis_size(order[stage]) - 1, rows, 128), BF16))
-        for stage in range(2):
-            scratch.append(pltpu.VMEM((rows_of(order, stage + 1), 128), BF16))
-    scratch += [
-        pltpu.SemaphoreType.DMA((9,)),
-        pltpu.SemaphoreType.DMA((9,)),
-        pltpu.SemaphoreType.DMA((len(JOBS), 6)),
-        pltpu.SemaphoreType.DMA((len(JOBS), 6)),
-    ]
+    for shape in ((12,), (len(GROUPS),), (9, 3), (9, NZ)):
+        scratch += [pltpu.SemaphoreType.DMA(shape)] * 2
     return pl.pallas_call(
         whole_kernel,
         out_shape=(
             jax.ShapeDtypeStruct(state, BF16),
             jax.ShapeDtypeStruct(state, F32),
             jax.ShapeDtypeStruct(state, F32),
-            jax.ShapeDtypeStruct((9 * UNIT, 128), BF16),
+            jax.ShapeDtypeStruct((9, NX, NY, NZ, SHARE, 128), BF16),
             jax.ShapeDtypeStruct((8, 256), F32),
             jax.ShapeDtypeStruct((TPD * PIX, 128), F32),
             jax.ShapeDtypeStruct((RIM, 128), F32),
@@ -620,7 +708,11 @@
     for o in range(9):
         fetch(o).wait()
         for k in range(4):
-            wide[o, :, k * 128 : (k + 1) * 128] = held[o, k].astype(F32)
+            pair, half = 2 * (k % 2), 64 * (k // 2)
+            wide[o, :, k * 128 : (k + 1) * 128] = jnp.concatenate(
+                [held[o, pair, :, half : half + 64], held[o, pair + 1, :, half : half + 64]],
+                axis=1,
+            ).astype(F32)
         put(o).start()
     hidden_out[...] = hidden[...]
     cell_out[...] = cell[...]
@@ -695,7 +787,7 @@
         [a.T for a in (edge_source, edge_code, corner_source, corner_code)],
     )
     hidden_new, cell_new, cell_grad, kernel_grad, bias_grad, input_grad, hidden_grad = finish(
-        hidden_new, cell_new, cell_grad, grad.reshape(9, 4, 256, 128), bias, inner, sides
+        hidden_new, cell_new, cell_grad, grad.reshape(9, NX, NY * NZ * SHARE, 128), bias, inner, sides
     )
     return (
         hidden_new,

time: 92.5 us -> 85.4 us (0.923); the launches traced: 92 us -> 83.7 us
  Pallas kernels: 91.3 us -> 83.1 us
    pallas_call x1, Pallas kernels: 86.2 us -> 77.9 us  [whole(): pl.pallas_call(whole_kernel, out_shape=(jax.ShapeDtypeStruct(state, BF16)...]
where the time goes in v3:
time: 85.4 us; the launch traced here: 83.7 us
  Pallas kernels  83.1 us (97%)
    pallas_call x1, Pallas kernels, whole(): pl.pallas_call(whole_kernel, out_shape=(jax.ShapeDtypeStruct(state, BF16)...  77.9 us
    pallas_call x1, Pallas kernels, finish(): pl.pallas_call(finish_kernel, out_shape=(jax.ShapeDtypeStruct(hidden.shap...  5.18 us

profile of v3, /device:TPU:32, one launch (start us, length us, event | category | flops | bytes accessed | tf_op | source)
XLA Modules:
  0.0 83.7 jit_solution(16116969667256794138)
XLA Ops:
  0.6 77.9 %whole.1 = (bf16[3,64,64]{2,1,0:T(8,128)(2,1)}, f32[3,64,64]{2,1,0:T(8,128)}, f32[3,64,64]{2,1,0:T(8,128)}, bf16[9,4,2,8,16,128]{5,4,3,2,1,0:T(8,128)(2,1)}, f32...) custom-call(bf16[3,64,64]{2,1,0:T(8,128)(2,1)} %inp.1, bf16[3,64,64]{2,1,0:T(8,128)(2,1)} %hid.1, ...), custom_call_target="tpu_custom_call" | custom-call | tf_op jit(solution)/shard_map/whole/pallas_call | solution.py:658
  78.5 5.2 %finish.1 = (bf16[3,64,64]{2,1,0:T(8,128)(2,1)}, f32[3,64,64]{2,1,0:T(8,128)}, f32[3,64,64]{2,1,0:T(8,128)}, f32[9,256,512]{2,1,0:T(8,128)}, f32[4,64]{1,0:T(4,1...) custom-call(bf16[3,64,64]{2,1,0:T(8,128)(2,1)} %get-tuple-element.21.hidden, ...), custom_call_target="tpu_custom_call" | custom-call | tf_op jit(solution)/shard_map/finish/pallas_call | solution.py:741

commit v4 on v3

--- a/solution.py
+++ b/solution.py
@@ -143,26 +143,41 @@
 
 
 def whole_kernel(
+    inp_hbm,
+    hid_hbm,
+    esrc_hbm,
+    ecode_hbm,
+    csrc_hbm,
+    ccode_hbm,
+    cell_prev_hbm,
+    bias_hbm,
+    hidden_up_hbm,
+    cell_up_hbm,
+    kern_hbm,
+    hidden_hbm,
+    cell_hbm,
+    cell_grad_hbm,
+    grad_hbm,
+    bias_sum_hbm,
+    inner_hbm,
+    side_hbm,
     inp,
     hid,
-    cell_prev,
-    kern_hbm,
-    gate_bias,
-    hidden_up,
-    cell_up,
     esrc,
     ecode,
     csrc,
     ccode,
+    cell_prev,
+    gate_bias,
+    hidden_up,
+    cell_up,
     hidden_out,
     cell_out,
     cell_grad_out,
-    grad_out,
     bias_out,
     inner_out,
     side_out,
     kern,
-    kern_sem,
     cells,
     field,
     rim,
@@ -173,8 +188,9 @@
     arrived,
     field_all,
     margin_all,
+    field_blocks,
+    margin_blocks,
     wide,
-    windows,
     accs,
     field_near,
     margin_near,
@@ -184,6 +200,7 @@
     turned_near,
     grad,
     grad_in,
+    grad_all,
     gauge,
     bias,
     dpad,
@@ -195,9 +212,8 @@
     slot_sum,
     slot_send,
     slot_in,
-    bias_in_q,
-    bias_mid,
-    bias_in_z,
+    slot_chooser,
+    bias_in,
     small_s,
     small_r,
     sum_s,
@@ -206,6 +222,9 @@
     all_r,
     ring_s,
     ring_r,
+    out_sems,
+    load_sems,
+    store_sems,
 ):
     q, y, x, z, c = position()
     to = peers()
@@ -214,9 +233,43 @@
         return lax.rem(lax.rem(q + d, NQ), NX)
 
     greeted = greet(to)
-    load = pltpu.make_async_copy(kern_hbm, kern, kern_sem)
-    load.start()
+    loads = [
+        pltpu.make_async_copy(far, near, load_sems.at[i])
+        for i, (far, near) in enumerate(
+            (
+                (inp_hbm, inp),
+                (hid_hbm, hid),
+                (esrc_hbm, esrc),
+                (ecode_hbm, ecode),
+                (csrc_hbm, csrc),
+                (ccode_hbm, ccode),
+                (cell_prev_hbm, cell_prev),
+                (bias_hbm, gate_bias),
+                (hidden_up_hbm, hidden_up),
+                (cell_up_hbm, cell_up),
+                (kern_hbm, kern),
+            )
+        )
+    ]
+    for load in loads:
+        load.start()
+    stores = [
+        pltpu.make_async_copy(near, far, store_sems.at[i])
+        for i, (near, far) in enumerate(
+            (
+                (hidden_out, hidden_hbm),
+                (cell_out, cell_hbm),
+                (cell_grad_out, cell_grad_hbm),
+                (inner_out, inner_hbm),
+                (side_out, side_hbm),
+                (bias_out, bias_sum_hbm),
+            )
+        )
+    ]
+    for load in loads[:2]:
+        load.wait()
     own_cells(inp, hid, cells, field, rim)
+    margin_in[:, MARGIN:128, :] = jnp.zeros((NQ, 128 - MARGIN, 128), BF16)
     pl.semaphore_wait(pltpu.get_barrier_semaphore(), greeted)
 
     for d in range(1, NZ):
@@ -225,6 +278,8 @@
         send(field, field_all.at[c], small_s.at[6], small_r.at[6], to["c"](d))
     table[z] = rim[...]
     field_all[c] = field[...]
+    for load in loads[2:6]:
+        load.wait()
     source_cells(esrc, ecode, csrc, ccode, by_tile, index)
 
     first = q * (NZ * RIM)
@@ -241,33 +296,38 @@
                 axis=1,
             )
         )
+    def lanes(ref, k):
+        pair, half = 2 * (k % 2), 64 * (k // 2)
+        return jnp.concatenate(
+            [ref[pair][:, half : half + 64], ref[pair + 1][:, half : half + 64]], axis=1
+        )
+
+    await_bytes(field_all.at[pl.ds(0, NC - 1)], small_r.at[6])
+    for k in range(4):
+        field_blocks[k] = lanes(field_all, k)
+    for d in range(1, NQ):
+        send(
+            field_blocks.at[quarter(d)],
+            field_near.at[d],
+            small_s.at[9],
+            small_r.at[9],
+            to["q"](d),
+        )
+    field_near[0] = field_blocks[x]
+    for k in range(4):
+        body = field_blocks[k].astype(F32)
+        for t in range(TPD):
+            base = t * 80
+            wide[1, k, base + 8 : base + 72, :] = body[t * PIX : (t + 1) * PIX]
+            wide[0, k, base + 9 : base + 72, :] = wide[1, k, base + 8 : base + 71, :]
+            wide[2, k, base + 8 : base + 71, :] = wide[1, k, base + 9 : base + 72, :]
+
     await_bytes(table.at[pl.ds(0, NZ - 1)], small_r.at[5])
     rims = table[...].reshape(NZ * RIM, 128)
     for d in list(range(1, NQ)) + [0]:
         picked[d] = nn(choosers[d], rims)[:MARGIN].astype(BF16)
         if d:
             send(picked.at[d], arrived.at[d - 1], small_s.at[7], small_r.at[7], to["q"](d))
-
-    def lanes(ref, k):
-        pair, half = 2 * (k % 2), 64 * (k // 2)
-        return jnp.concatenate(
-            [ref[pair][:, half : half + 64], ref[pair + 1][:, half : half + 64]], axis=1
-        ).astype(F32)
-
-    await_bytes(field_all.at[pl.ds(0, NC - 1)], small_r.at[6])
-    for d in range(1, NQ):
-        send(
-            field_all.at[quarter(d)],
-            field_near.at[d],
-            small_s.at[9],
-            small_r.at[9],
-            to["q"](d),
-        )
-    field_near[0] = field_all[x]
-    for k in range(4):
-        body = lanes(field_all, k)
-        for t in range(TPD):
-            wide[1, k, t * 80 + 8 : t * 80 + 72, :] = body[t * PIX : (t + 1) * PIX]
 
     await_bytes(arrived, small_r.at[7])
     total = picked[0].astype(F32)
@@ -276,43 +336,52 @@
     margin_all[c] = total.astype(BF16)
     for d in range(1, NC):
         send(margin_all.at[c], margin_all.at[c], small_s.at[8], small_r.at[8], to["c"](d))
-    load.wait()
+    for load in loads[6:]:
+        load.wait()
     await_bytes(margin_all.at[pl.ds(0, NC - 1)], small_r.at[8])
+    for k in range(4):
+        margin_blocks[k] = lanes(margin_all, k)
     for d in range(1, NQ):
         send(
-            margin_all.at[quarter(d)],
+            margin_blocks.at[quarter(d)],
             margin_near.at[d],
             small_s.at[10],
             small_r.at[10],
             to["q"](d),
         )
-    margin_near[0] = margin_all[x]
+    margin_near[0] = margin_blocks[x]
 
     for k in range(4):
-        margin = lanes(margin_all, k)
-        for t in range(TPD):
-            base, at = t * 80, t * 32
-            wide[1, k, base : base + 8, :] = margin[at : at + 8]
-            wide[1, k, base + 72 : base + 80, :] = margin[at + 16 : at + 24]
-        wide[0, k, 1:BODY, :] = wide[1, k, 0 : BODY - 1, :]
-        wide[2, k, 0 : BODY - 1, :] = wide[1, k, 1:BODY, :]
+        margin = margin_blocks[k].astype(F32)
+        left, right = wide.at[0, k], wide.at[2, k]
         for t in range(TPD):
             base, at, corner = t * 80, t * 32, RIM + t * 4
-            left, right = wide.at[0, k], wide.at[2, k]
+            for row, side in ((base, at), (base + 72, at + 16)):
+                wide[1, k, row : row + 8, :] = margin[side : side + 8]
+                left[row + 1 : row + 8, :] = margin[side : side + 7]
+                right[row : row + 7, :] = margin[side + 1 : side + 8]
             left[base : base + 1, :] = margin[corner : corner + 1]
             left[pl.ds(base + 8, 8, stride=8), :] = margin[at + 24 : at + 32]
             left[base + 72 : base + 73, :] = margin[corner + 3 : corner + 4]
             right[base + 7 : base + 8, :] = margin[corner + 1 : corner + 2]
             right[pl.ds(base + 15, 8, stride=8), :] = margin[at + 8 : at + 16]
             right[base + 79 : base + 80, :] = margin[corner + 2 : corner + 3]
-    for o in range(9):
-        a, b = o // 3, o % 3
-        for k in range(4):
-            for t in range(TPD):
-                base = t * 80 + a * 8
-                windows[o, t * PIX : (t + 1) * PIX, k * 128 : (k + 1) * 128] = wide[
-                    b, k, base : base + PIX, :
-                ].astype(BF16)
+
+    def window(o):
+        start = (o // 3) * 8
+        return jnp.concatenate(
+            [
+                jnp.concatenate(
+                    [
+                        wide[o % 3, k, t * 80 + start : t * 80 + start + PIX, :]
+                        for t in range(TPD)
+                    ],
+                    axis=0,
+                ).astype(BF16)
+                for k in range(4)
+            ],
+            axis=1,
+        )
 
     def gate(k):
         column = jnp.broadcast_to(gate_bias[k : k + 1, :], (64, 64)).T
@@ -320,7 +389,7 @@
 
     gates = jnp.concatenate([gate(k) for k in range(4)], axis=0)
     for o in range(9):
-        gates = gates + nt(kern[o], windows[o])
+        gates = gates + nt(kern[o], window(o))
     in_gate = jax.nn.sigmoid(gates[0:64])
     forget = jax.nn.sigmoid(gates[64:128])
     cand = jnp.tanh(gates[128:192])
@@ -389,22 +458,13 @@
                 [one[:, half], two[:, half]], axis=1
             ).astype(BF16)
             start += rows
-    for d in range(1, NC):
-        send(
-            dpad.at[lax.rem(c + d, NC)],
-            dpad_in.at[d - 1],
-            small_s.at[0],
-            small_r.at[0],
-            to["c"](d),
-        )
-    bias[...] = nt(jnp.ones((8, TPD * PIX), BF16), dgates)
-    for d in range(1, NQ):
-        send(bias, bias_in_q.at[d - 1], small_s.at[1], small_r.at[1], to["q"](d))
     for t in range(TPD):
         at = slice(t * PIX, (t + 1) * PIX)
         hidden_out[t] = hidden_new[:, at]
         cell_out[t] = cell_new[:, at]
         cell_grad_out[t] = cell_grad[:, at]
+    for store in stores[:3]:
+        store.start()
 
     await_bytes(field_near.at[pl.ds(0, NQ - 1)], small_r.at[9])
     await_bytes(margin_near.at[pl.ds(0, NQ - 1)], small_r.at[10])
@@ -439,6 +499,9 @@
     lax.fori_loop(0, NQ, windows_of, 0)
     await_bytes(turned_near.at[pl.ds(0, NQ - 1)], small_r.at[11])
     near = nt(eye(128), turned_near[...].reshape(NQ * TPD * PIX, 128)).astype(BF16)
+    bias[...] = nt(jnp.ones((8, NQ * TPD * PIX), BF16), near)
+    for d in range(1, NZ):
+        send(bias, bias_in.at[d - 1], small_s.at[1], small_r.at[1], to["z"](d))
     for g, (low, high) in enumerate(GROUPS):
         product = nn(near, windows_near[:, low * 128 : high * 128]).astype(BF16)
         for o in range(low, high):
@@ -453,6 +516,14 @@
                 to["z"](d),
             )
 
+    for d in range(1, NC):
+        send(
+            dpad.at[lax.rem(c + d, NC)],
+            dpad_in.at[d - 1],
+            small_s.at[0],
+            small_r.at[0],
+            to["c"](d),
+        )
     await_bytes(dpad_in, small_r.at[0])
     total = dpad[c].astype(F32)
     for d in range(NC - 1):
@@ -471,19 +542,80 @@
         margin_own[corner + 2 : corner + 3, :] = dsum[right + col + 9 : right + col + 10, :]
         margin_own[corner + 3 : corner + 4, :] = dsum[left + col + 9 : left + col + 10, :]
         inner_out[t * PIX : (t + 1) * PIX, :] = dsum[base + 8 : base + 72, :]
+    stores[3].start()
     margin_send[...] = margin_own[...].astype(BF16)
     for d in range(1, NQ):
-        send(margin_send, margin_in.at[d - 1], small_s.at[2], small_r.at[2], to["q"](d))
-
-    choosers = []
+        send(
+            margin_send,
+            margin_in.at[d, pl.ds(0, MARGIN)],
+            small_s.at[2],
+            small_r.at[2],
+            to["q"](d),
+        )
+    margin_in[0, 0:MARGIN, :] = margin_send[...]
     for d in range(NQ):
-        row = index[pl.ds(lax.rem(q + NQ - d, NQ) * NZ + z, 1), :][:, :MARGIN]
-        chooser = (iota((NZ * RIM, MARGIN), 0) == row - first).astype(F32).astype(BF16)
-        choosers.append(chooser)
-    await_bytes(margin_in, small_r.at[2])
-    sums = nn(choosers[0], margin_send[...])
-    for d in range(1, NQ):
-        sums += nn(choosers[d], margin_in[d - 1])
+        row = index[pl.ds(lax.rem(q + NQ - d, NQ) * NZ + z, 1), :]
+        chooser = (iota((NZ * RIM, 128), 0) == row - first).astype(F32).astype(BF16)
+        slot_chooser[:, d * 128 : (d + 1) * 128] = chooser
+
+    def box(o, full, at_z=None):
+        return grad_all.at[
+            o,
+            slice(None) if "x" in full else x,
+            slice(None) if "y" in full else y,
+            slice(None) if "z" in full else (z if at_z is None else at_z),
+        ]
+
+    def box_rows(full):
+        rows = SHARE
+        for axis in full:
+            rows *= axis_size(axis)
+        return rows
+
+    def bytes_of(rows):
+        return gauge.at[pl.ds(0, rows)]
+
+    def on_ring(o, stage):
+        return stage == 2 and ORDERS[o][2] == "z"
+
+    def ring_send(o, step, side):
+        share = lax.rem(z + NZ + (1 - step if side == 0 else step - 1), NZ)
+        mine = box(o, "xy", share)
+        at = (o, side * (NZ // 2) + step - 1)
+        send(mine, mine, ring_s.at[at], ring_r.at[at], to["z"](1 if side == 0 else NZ - 1))
+
+    def ring_wait(o, step, side):
+        await_bytes(bytes_of(box_rows("xy")), ring_r.at[o, side * (NZ // 2) + step - 1])
+
+    def gather(o, stage):
+        if on_ring(o, stage):
+            for side in range(2):
+                ring_send(o, 1, side)
+            return
+        axis, full = ORDERS[o][stage], ORDERS[o][:stage]
+        mine = box(o, full)
+        for d in range(1, axis_size(axis)):
+            send(mine, mine, all_s.at[o, stage], all_r.at[o, stage], to[axis](d))
+
+    def stage_bytes(o, stage):
+        axis, full = ORDERS[o][stage], ORDERS[o][:stage]
+        return bytes_of(box_rows(full) * (axis_size(axis) - 1))
+
+    def gathered(o, stage):
+        await_bytes(stage_bytes(o, stage), all_r.at[o, stage])
+
+    for g, (low, high) in enumerate(GROUPS):
+        some = pl.ds(low, high - low)
+        await_bytes(grad_in.at[:, some], sum_r.at[g])
+        total = grad[some, pl.ds(pl.multiple_of(z * SHARE, SHARE), SHARE), :].astype(F32)
+        for d in range(NZ - 1):
+            total += grad_in[d, some].astype(F32)
+        for o in range(low, high):
+            grad_all[o, x, y, z] = total[o - low].astype(BF16)
+            gather(o, 0)
+
+    await_bytes(margin_in.at[pl.ds(1, NQ - 1), pl.ds(0, MARGIN)], small_r.at[2])
+    sums = nn(slot_chooser[...], margin_in[...].reshape(NQ * 128, 128))
     slot_sum[...] = sums.reshape(NZ, RIM, 128)
     slot_send[...] = slot_sum[...].astype(BF16)
     for d in range(1, NZ):
@@ -494,85 +626,26 @@
             small_r.at[3],
             to["z"](d),
         )
-    await_bytes(bias_in_q, small_r.at[1])
+    await_bytes(bias_in, small_r.at[1])
     total = bias[...]
-    for d in range(NQ - 1):
-        total += bias_in_q[d]
-    bias_mid[...] = total
-    for d in range(1, NZ):
-        send(bias_mid, bias_in_z.at[d - 1], small_s.at[4], small_r.at[4], to["z"](d))
-
-    def box(o, full, at_z=None):
-        return grad_out.at[
-            o,
-            slice(None) if "x" in full else x,
-            slice(None) if "y" in full else y,
-            slice(None) if "z" in full else (z if at_z is None else at_z),
-        ]
-
-    def box_rows(full):
-        rows = SHARE
-        for axis in full:
-            rows *= axis_size(axis)
-        return rows
-
-    def bytes_of(rows):
-        return gauge.at[pl.ds(0, rows)]
-
-    def on_ring(o, stage):
-        return stage == 2 and ORDERS[o][2] == "z"
-
-    def ring_send(o, step, side):
-        share = lax.rem(z + NZ + (1 - step if side == 0 else step - 1), NZ)
-        mine = box(o, "xy", share)
-        at = (o, side * (NZ // 2) + step - 1)
-        send(mine, mine, ring_s.at[at], ring_r.at[at], to["z"](1 if side == 0 else NZ - 1))
-
-    def ring_wait(o, step, side):
-        await_bytes(bytes_of(box_rows("xy")), ring_r.at[o, side * (NZ // 2) + step - 1])
-
-    def gather(o, stage):
-        if on_ring(o, stage):
-            for side in range(2):
-                ring_send(o, 1, side)
-            return
-        axis, full = ORDERS[o][stage], ORDERS[o][:stage]
-        mine = box(o, full)
-        for d in range(1, axis_size(axis)):
-            send(mine, mine, all_s.at[o, stage], all_r.at[o, stage], to[axis](d))
-
-    def stage_bytes(o, stage):
-        axis, full = ORDERS[o][stage], ORDERS[o][:stage]
-        return bytes_of(box_rows(full) * (axis_size(axis) - 1))
-
-    def gathered(o, stage):
-        await_bytes(stage_bytes(o, stage), all_r.at[o, stage])
-
-    for g, (low, high) in enumerate(GROUPS):
-        some = pl.ds(low, high - low)
-        await_bytes(grad_in.at[:, some], sum_r.at[g])
-        total = grad[some, pl.ds(pl.multiple_of(z * SHARE, SHARE), SHARE), :].astype(F32)
-        for d in range(NZ - 1):
-            total += grad_in[d, some].astype(F32)
-        for o in range(low, high):
-            grad_out[o, x, y, z] = total[o - low].astype(BF16)
-            gather(o, 0)
-
+    for d in range(NZ - 1):
+        total += bias_in[d]
+    bias_out[y] = total
+    send(bias_out.at[y], bias_out.at[y], small_s.at[4], small_r.at[4], to["y"](1))
+
+    def put(o):
+        return pltpu.make_async_copy(grad_all.at[o], grad_hbm.at[o], out_sems.at[o])
+
+    for stage in (0, 1):
+        for o in range(9):
+            gathered(o, stage)
+            gather(o, stage + 1)
     await_bytes(slot_in, small_r.at[3])
     total = slot_sum[z]
     for d in range(NZ - 1):
         total += slot_in[d].astype(F32)
     side_out[...] = total
-    await_bytes(bias_in_z, small_r.at[4])
-    total = bias_mid[...]
-    for d in range(NZ - 1):
-        total += bias_in_z[d]
-    bias_out[...] = total
-
-    for stage in (0, 1):
-        for o in range(9):
-            gathered(o, stage)
-            gather(o, stage + 1)
+    stores[4].start()
     for step in range(1, NZ // 2 + 1):
         for o in range(9):
             if on_ring(o, 2):
@@ -581,15 +654,23 @@
                         ring_wait(o, step, side)
                     if step < ring_steps(o)[side]:
                         ring_send(o, step + 1, side)
+                if step == NZ // 2:
+                    put(o).start()
+            elif step == 3:
+                gathered(o, 2)
+                put(o).start()
+    await_bytes(bias, small_r.at[4])
+    stores[5].start()
+    for store in stores:
+        store.wait()
     for o in range(9):
-        if not on_ring(o, 2):
-            gathered(o, 2)
+        put(o).wait()
 
     await_bytes(dpad_in, small_s.at[0])
-    await_bytes(bias_in_q, small_s.at[1])
-    await_bytes(margin_in, small_s.at[2])
+    await_bytes(bias_in, small_s.at[1])
+    await_bytes(margin_in.at[pl.ds(1, NQ - 1), pl.ds(0, MARGIN)], small_s.at[2])
     await_bytes(slot_in, small_s.at[3])
-    await_bytes(bias_in_z, small_s.at[4])
+    await_bytes(bias, small_s.at[4])
     await_bytes(table.at[pl.ds(0, NZ - 1)], small_s.at[5])
     await_bytes(field_all.at[pl.ds(0, NC - 1)], small_s.at[6])
     await_bytes(arrived, small_s.at[7])
@@ -611,12 +692,23 @@
 
 
 def whole(inp, hid, cell_prev, kern, gate_bias, hidden_up, cell_up, lists):
-    vmem = pl.BlockSpec(memory_space=pltpu.VMEM)
+    hbm = pl.BlockSpec(memory_space=pl.ANY)
     state = cell_prev.shape
     devices = NQ * NZ
-    scratch = [
+    operands = (inp, hid, *lists, cell_prev, gate_bias, hidden_up, cell_up, kern)
+    results = (
+        jax.ShapeDtypeStruct(state, BF16),
+        jax.ShapeDtypeStruct(state, F32),
+        jax.ShapeDtypeStruct(state, F32),
+        jax.ShapeDtypeStruct((9, NX, NY, NZ, SHARE, 128), BF16),
+        jax.ShapeDtypeStruct((NY, 8, 128), F32),
+        jax.ShapeDtypeStruct((TPD * PIX, 128), F32),
+        jax.ShapeDtypeStruct((RIM, 128), F32),
+    )
+    scratch = [pltpu.VMEM(a.shape, a.dtype) for a in operands[:-1]]
+    scratch += [pltpu.VMEM(a.shape, a.dtype) for a in results[:3] + results[4:]]
+    scratch += [
         pltpu.VMEM(kern.shape, BF16),
-        pltpu.SemaphoreType.DMA,
         pltpu.VMEM((TPD * PIX, 128), F32),
         pltpu.VMEM((TPD * PIX, 128), BF16),
         pltpu.VMEM((RIM, 128), BF16),
@@ -627,8 +719,9 @@
         pltpu.VMEM((NQ - 1, MARGIN, 128), BF16),
         pltpu.VMEM((NC, TPD * PIX, 128), BF16),
         pltpu.VMEM((NC, MARGIN, 128), BF16),
+        pltpu.VMEM((4, TPD * PIX, 128), BF16),
+        pltpu.VMEM((4, MARGIN, 128), BF16),
         pltpu.VMEM((3, 4, BODY, 128), F32),
-        pltpu.VMEM((9, TPD * PIX, 512), BF16),
         pltpu.VMEM((3, 4, 8 + BODY + 32, 128), F32),
         pltpu.VMEM((NQ, TPD * PIX, 128), BF16),
         pltpu.VMEM((NQ, MARGIN, 128), BF16),
@@ -638,64 +731,67 @@
         pltpu.VMEM((NQ, TPD * PIX, 128), BF16),
         pltpu.VMEM((9, 128, 128), BF16),
         pltpu.VMEM((NZ - 1, 9, SHARE, 128), BF16),
+        pltpu.VMEM((9, NX, NY, NZ, SHARE, 128), BF16),
         pltpu.VMEM((1024, 128), BF16),
-        pltpu.VMEM((8, 256), F32),
+        pltpu.VMEM((8, 128), F32),
         pltpu.VMEM((NC, DROWS, 128), BF16),
         pltpu.VMEM((NC - 1, DROWS, 128), BF16),
         pltpu.VMEM((DROWS, 128), F32),
         pltpu.VMEM((MARGIN, 128), F32),
         pltpu.VMEM((MARGIN, 128), BF16),
-        pltpu.VMEM((NQ - 1, MARGIN, 128), BF16),
+        pltpu.VMEM((NQ, 128, 128), BF16),
         pltpu.VMEM((NZ, RIM, 128), F32),
         pltpu.VMEM((NZ, RIM, 128), BF16),
         pltpu.VMEM((NZ - 1, RIM, 128), BF16),
-        pltpu.VMEM((NQ - 1, 8, 256), F32),
-        pltpu.VMEM((8, 256), F32),
-        pltpu.VMEM((NZ - 1, 8, 256), F32),
+        pltpu.VMEM((NZ * RIM, NQ * 128), BF16),
+        pltpu.VMEM((NZ - 1, 8, 128), F32),
     ]
     for shape in ((12,), (len(GROUPS),), (9, 3), (9, NZ)):
         scratch += [pltpu.SemaphoreType.DMA(shape)] * 2
+    for count in (9, len(operands), len(results) - 1):
+        scratch.append(pltpu.SemaphoreType.DMA((count,)))
     return pl.pallas_call(
         whole_kernel,
-        out_shape=(
-            jax.ShapeDtypeStruct(state, BF16),
-            jax.ShapeDtypeStruct(state, F32),
-            jax.ShapeDtypeStruct(state, F32),
-            jax.ShapeDtypeStruct((9, NX, NY, NZ, SHARE, 128), BF16),
-            jax.ShapeDtypeStruct((8, 256), F32),
-            jax.ShapeDtypeStruct((TPD * PIX, 128), F32),
-            jax.ShapeDtypeStruct((RIM, 128), F32),
-        ),
-        in_specs=[vmem] * 3 + [pl.BlockSpec(memory_space=pl.ANY)] + [vmem] * 7,
-        out_specs=(vmem,) * 7,
+        out_shape=results,
+        in_specs=[hbm] * len(operands),
+        out_specs=(hbm,) * len(results),
         scratch_shapes=scratch,
         compiler_params=pltpu.CompilerParams(
             collective_id=0, has_side_effects=True, vmem_limit_bytes=VMEM_LIMIT
         ),
         name="whole",
-    )(inp, hid, cell_prev, kern, gate_bias, hidden_up, cell_up, *lists)
+    )(*operands)
 
 
 def finish_kernel(
-    hidden,
-    cell,
-    cell_grad,
+    hidden_hbm,
+    cell_hbm,
+    cell_grad_hbm,
     grad,
-    bias,
-    inner,
-    sides,
+    bias_hbm,
+    inner_hbm,
+    sides_hbm,
     hidden_out,
     cell_out,
     cell_grad_out,
     grad_out,
+    bias_out_hbm,
+    input_out_hbm,
+    prior_out_hbm,
+    held,
+    wide,
+    bias,
+    cells,
+    sides,
+    hidden,
+    cell,
+    cell_grad,
     bias_out,
     input_out,
     prior_out,
-    held,
-    wide,
-    cells,
     sems_in,
     sems_out,
+    sems,
 ):
     def fetch(o):
         return pltpu.make_async_copy(grad.at[o], held.at[o], sems_in.at[o])
@@ -703,23 +799,41 @@
     def put(o):
         return pltpu.make_async_copy(wide.at[o], grad_out.at[o], sems_out.at[o])
 
-    for o in range(9):
+    small = [
+        pltpu.make_async_copy(source, target, sems.at[i])
+        for i, (source, target) in enumerate(
+            (
+                (bias_hbm, bias),
+                (inner_hbm, cells),
+                (sides_hbm, sides),
+                (hidden_hbm, hidden),
+                (cell_hbm, cell),
+                (cell_grad_hbm, cell_grad),
+                (hidden, hidden_out),
+                (cell, cell_out),
+                (cell_grad, cell_grad_out),
+                (bias_out, bias_out_hbm),
+                (input_out, input_out_hbm),
+                (prior_out, prior_out_hbm),
+            )
+        )
+    ]
+    fetch(0).start()
+    for copy in small[:6]:
+        copy.start()
+    for o in range(1, 9):
         fetch(o).start()
     for o in range(9):
         fetch(o).wait()
         for k in range(4):
-            pair, half = 2 * (k % 2), 64 * (k // 2)
-            wide[o, :, k * 128 : (k + 1) * 128] = jnp.concatenate(
-                [held[o, pair, :, half : half + 64], held[o, pair + 1, :, half : half + 64]],
-                axis=1,
-            ).astype(F32)
+            wide[o, :, k * 128 : (k + 1) * 128] = held[o, k].astype(F32)
         put(o).start()
-    hidden_out[...] = hidden[...]
-    cell_out[...] = cell[...]
-    cell_grad_out[...] = cell_grad[...]
+    for copy in small[:6]:
+        copy.wait()
+    for copy in small[6:9]:
+        copy.start()
     for k in range(4):
-        bias_out[k : k + 1, :] = bias[0:1, k * 64 : (k + 1) * 64]
-    cells[...] = inner[...]
+        bias_out[k : k + 1, :] = bias[k // 2, 0:1, (k % 2) * 64 : (k % 2 + 1) * 64]
     for t in range(TPD):
         base, at = t * PIX, t * 32
         cells[base : base + 8, :] += sides[at : at + 8, :]
@@ -732,31 +846,45 @@
         turned = nt(ident, rounded).astype(BF16)
         input_out[t] = turned[0:64]
         prior_out[t] = turned[64:128]
+    for copy in small[9:]:
+        copy.start()
+    for copy in small[6:]:
+        copy.wait()
     for o in range(9):
         put(o).wait()
 
 
 def finish(hidden, cell, cell_grad, grad, bias, inner, sides):
-    vmem, hbm = pl.BlockSpec(memory_space=pltpu.VMEM), pl.BlockSpec(memory_space=pl.ANY)
+    hbm = pl.BlockSpec(memory_space=pl.ANY)
+    state = hidden.shape
     return pl.pallas_call(
         finish_kernel,
         out_shape=(
-            jax.ShapeDtypeStruct(hidden.shape, BF16),
-            jax.ShapeDtypeStruct(hidden.shape, F32),
-            jax.ShapeDtypeStruct(hidden.shape, F32),
+            jax.ShapeDtypeStruct(state, BF16),
+            jax.ShapeDtypeStruct(state, F32),
+            jax.ShapeDtypeStruct(state, F32),
             jax.ShapeDtypeStruct((9, 256, 512), F32),
             jax.ShapeDtypeStruct((4, 64), F32),
-            jax.ShapeDtypeStruct(hidden.shape, BF16),
-            jax.ShapeDtypeStruct(hidden.shape, BF16),
+            jax.ShapeDtypeStruct(state, BF16),
+            jax.ShapeDtypeStruct(state, BF16),
         ),
-        in_specs=[vmem] * 3 + [hbm] + [vmem] * 3,
-        out_specs=(vmem,) * 3 + (hbm,) + (vmem,) * 3,
+        in_specs=[hbm] * 7,
+        out_specs=(hbm,) * 7,
         scratch_shapes=[
             pltpu.VMEM(grad.shape, BF16),
             pltpu.VMEM((9, 256, 512), F32),
+            pltpu.VMEM(bias.shape, F32),
             pltpu.VMEM(inner.shape, F32),
+            pltpu.VMEM(sides.shape, F32),
+            pltpu.VMEM(state, BF16),
+            pltpu.VMEM(state, F32),
+            pltpu.VMEM(state, F32),
+            pltpu.VMEM((4, 64), F32),
+            pltpu.VMEM(state, BF16),
+            pltpu.VMEM(state, BF16),
             pltpu.SemaphoreType.DMA((9,)),
             pltpu.SemaphoreType.DMA((9,)),
+            pltpu.SemaphoreType.DMA((12,)),
         ],
         compiler_params=pltpu.CompilerParams(vmem_limit_bytes=VMEM_LIMIT),
         name="finish",

time: 85.4 us -> 78 us (0.913); the launches traced: 83.7 us -> 77.3 us
  Pallas kernels: 83.1 us -> 76.6 us
    pallas_call x2, Pallas kernels: 83.1 us -> 76.6 us  [the longest x1 73.1 us: whole(): pl.pallas_call(whole_kernel, out_shape=results, in_specs=[hbm] * len(oper...]
where the time goes in v4:
time: 78 us; the launch traced here: 77.3 us
  Pallas kernels  76.6 us (98%)
    pallas_call x1, Pallas kernels, whole(): pl.pallas_call(whole_kernel, out_shape=results, in_specs=[hbm] * len(oper...  73.1 us
    pallas_call x1, Pallas kernels, finish(): pl.pallas_call(finish_kernel, out_shape=(jax.ShapeDtypeStruct(state, BF16...  3.54 us

profile of v4, /device:TPU:32, one launch (start us, length us, event | category | flops | bytes accessed | tf_op | source)
XLA Modules:
  0.0 77.3 jit_solution(6109150575663003299)
XLA Ops:
  0.6 73.1 %whole.1 = (bf16[3,64,64]{2,1,0:T(8,128)(2,1)}, f32[3,64,64]{2,1,0:T(8,128)}, f32[3,64,64]{2,1,0:T(8,128)}, bf16[9,4,2,8,16,128]{5,4,3,2,1,0:T(8,128)(2,1)}, f32...) custom-call(bf16[3,64,64]{2,1,0:T(8,128)(2,1)} %inp_hbm.1, bf16[3,64,64]{2,1,0:T(8,128)(2,1)} %hid_hbm.1, ...), custom_call_target="tpu_custom_call" | custom-call | tf_op jit(solution)/shard_map/whole/pallas_call | solution.py:753
  73.7 3.5 %finish.1 = (bf16[3,64,64]{2,1,0:T(8,128)(2,1)}, f32[3,64,64]{2,1,0:T(8,128)}, f32[3,64,64]{2,1,0:T(8,128)}, f32[9,256,512]{2,1,0:T(8,128)}, f32[4,64]{1,0:T(4,1...) custom-call(bf16[3,64,64]{2,1,0:T(8,128)(2,1)} %get-tuple-element.21.hidden_hbm, ...), custom_call_target="tpu_custom_call" | custom-call | tf_op jit(solution)/shard_map/finish/pallas_call | solution.py:860

commit v5 on v4

--- a/solution.py
+++ b/solution.py
@@ -20,7 +20,23 @@
 DROWS = BODY + 64
 SHARE = 16
 GROUPS = ((0, 3), (3, 6), (6, 9))
-ORDERS = ("yxz", "zyx", "yxz", "zxy", "yxz", "zyx", "yxz", "zxy", "zyx")
+JOBS = ((0, 3, "yxz"), (3, 6, "zxy"), (6, 9, "zyx"))
+SCHEDULE = (
+    ("sum", 0),
+    ("sum", 1),
+    ("sum", 2),
+    ("slots",),
+    ("go", 0, 0),
+    ("go", 1, 0),
+    ("go", 2, 0),
+    ("go", 0, 1),
+    ("go", 1, 1),
+    ("go", 2, 1),
+    ("ring", 1),
+    ("ring", 2),
+    ("ring", 3),
+    ("ring", 4),
+)
 VMEM_LIMIT = 56 * 1024 * 1024
 
 
@@ -90,8 +106,13 @@
     return {"x": NX, "y": NY, "z": NZ}[axis]
 
 
-def ring_steps(o):
-    return (NZ // 2, NZ // 2 - 1) if o % 2 == 0 else (NZ // 2 - 1, NZ // 2)
+def jobs_of(group):
+    low, high = GROUPS[group]
+    return [j for j, job in enumerate(JOBS) if low <= job[0] < high]
+
+
+def ring_steps(j):
+    return (NZ // 2, NZ // 2 - 1) if j % 2 == 0 else (NZ // 2 - 1, NZ // 2)
 
 
 def own_cells(inp, hid, cells, field, rim):
@@ -498,6 +519,14 @@
 
     lax.fori_loop(0, NQ, windows_of, 0)
     await_bytes(turned_near.at[pl.ds(0, NQ - 1)], small_r.at[11])
+    for d in range(1, NC):
+        send(
+            dpad.at[lax.rem(c + d, NC)],
+            dpad_in.at[d - 1],
+            small_s.at[0],
+            small_r.at[0],
+            to["c"](d),
+        )
     near = nt(eye(128), turned_near[...].reshape(NQ * TPD * PIX, 128)).astype(BF16)
     bias[...] = nt(jnp.ones((8, NQ * TPD * PIX), BF16), near)
     for d in range(1, NZ):
@@ -516,14 +545,6 @@
                 to["z"](d),
             )
 
-    for d in range(1, NC):
-        send(
-            dpad.at[lax.rem(c + d, NC)],
-            dpad_in.at[d - 1],
-            small_s.at[0],
-            small_r.at[0],
-            to["c"](d),
-        )
     await_bytes(dpad_in, small_r.at[0])
     total = dpad[c].astype(F32)
     for d in range(NC - 1):
@@ -558,16 +579,16 @@
         chooser = (iota((NZ * RIM, 128), 0) == row - first).astype(F32).astype(BF16)
         slot_chooser[:, d * 128 : (d + 1) * 128] = chooser
 
-    def box(o, full, at_z=None):
+    def box(j, full, at_z=None):
         return grad_all.at[
-            o,
+            pl.ds(JOBS[j][0], JOBS[j][1] - JOBS[j][0]),
             slice(None) if "x" in full else x,
             slice(None) if "y" in full else y,
             slice(None) if "z" in full else (z if at_z is None else at_z),
         ]
 
-    def box_rows(full):
-        rows = SHARE
+    def box_rows(j, full):
+        rows = SHARE * (JOBS[j][1] - JOBS[j][0])
         for axis in full:
             rows *= axis_size(axis)
         return rows
@@ -575,36 +596,37 @@
     def bytes_of(rows):
         return gauge.at[pl.ds(0, rows)]
 
-    def on_ring(o, stage):
-        return stage == 2 and ORDERS[o][2] == "z"
-
-    def ring_send(o, step, side):
+    def on_ring(j, stage):
+        return stage == 2 and JOBS[j][2][2] == "z"
+
+    def ring_send(j, step, side):
         share = lax.rem(z + NZ + (1 - step if side == 0 else step - 1), NZ)
-        mine = box(o, "xy", share)
-        at = (o, side * (NZ // 2) + step - 1)
+        mine = box(j, "xy", share)
+        at = (j, side * (NZ // 2) + step - 1)
         send(mine, mine, ring_s.at[at], ring_r.at[at], to["z"](1 if side == 0 else NZ - 1))
 
-    def ring_wait(o, step, side):
-        await_bytes(bytes_of(box_rows("xy")), ring_r.at[o, side * (NZ // 2) + step - 1])
-
-    def gather(o, stage):
-        if on_ring(o, stage):
+    def ring_wait(j, step, side):
+        await_bytes(bytes_of(box_rows(j, "xy")), ring_r.at[j, side * (NZ // 2) + step - 1])
+
+    def gather(j, stage):
+        if on_ring(j, stage):
             for side in range(2):
-                ring_send(o, 1, side)
+                ring_send(j, 1, side)
             return
-        axis, full = ORDERS[o][stage], ORDERS[o][:stage]
-        mine = box(o, full)
+        axis, full = JOBS[j][2][stage], JOBS[j][2][:stage]
+        mine = box(j, full)
         for d in range(1, axis_size(axis)):
-            send(mine, mine, all_s.at[o, stage], all_r.at[o, stage], to[axis](d))
-
-    def stage_bytes(o, stage):
-        axis, full = ORDERS[o][stage], ORDERS[o][:stage]
-        return bytes_of(box_rows(full) * (axis_size(axis) - 1))
-
-    def gathered(o, stage):
-        await_bytes(stage_bytes(o, stage), all_r.at[o, stage])
-
-    for g, (low, high) in enumerate(GROUPS):
+            send(mine, mine, all_s.at[j, stage], all_r.at[j, stage], to[axis](d))
+
+    def stage_bytes(j, stage):
+        axis, full = JOBS[j][2][stage], JOBS[j][2][:stage]
+        return bytes_of(box_rows(j, full) * (axis_size(axis) - 1))
+
+    def gathered(j, stage):
+        await_bytes(stage_bytes(j, stage), all_r.at[j, stage])
+
+    def sum_over_z(g):
+        low, high = GROUPS[g]
         some = pl.ds(low, high - low)
         await_bytes(grad_in.at[:, some], sum_r.at[g])
         total = grad[some, pl.ds(pl.multiple_of(z * SHARE, SHARE), SHARE), :].astype(F32)
@@ -612,59 +634,68 @@
             total += grad_in[d, some].astype(F32)
         for o in range(low, high):
             grad_all[o, x, y, z] = total[o - low].astype(BF16)
-            gather(o, 0)
-
-    await_bytes(margin_in.at[pl.ds(1, NQ - 1), pl.ds(0, MARGIN)], small_r.at[2])
-    sums = nn(slot_chooser[...], margin_in[...].reshape(NQ * 128, 128))
-    slot_sum[...] = sums.reshape(NZ, RIM, 128)
-    slot_send[...] = slot_sum[...].astype(BF16)
-    for d in range(1, NZ):
-        send(
-            slot_send.at[lax.rem(z + d, NZ)],
-            slot_in.at[d - 1],
-            small_s.at[3],
-            small_r.at[3],
-            to["z"](d),
-        )
-    await_bytes(bias_in, small_r.at[1])
-    total = bias[...]
-    for d in range(NZ - 1):
-        total += bias_in[d]
-    bias_out[y] = total
-    send(bias_out.at[y], bias_out.at[y], small_s.at[4], small_r.at[4], to["y"](1))
-
-    def put(o):
-        return pltpu.make_async_copy(grad_all.at[o], grad_hbm.at[o], out_sems.at[o])
-
-    for stage in (0, 1):
-        for o in range(9):
-            gathered(o, stage)
-            gather(o, stage + 1)
+        for j in jobs_of(g):
+            gather(j, 0)
+
+    def advance(g, stage):
+        for j in jobs_of(g):
+            gathered(j, stage)
+            gather(j, stage + 1)
+
+    def slots():
+        await_bytes(margin_in.at[pl.ds(1, NQ - 1), pl.ds(0, MARGIN)], small_r.at[2])
+        sums = nn(slot_chooser[...], margin_in[...].reshape(NQ * 128, 128))
+        slot_sum[...] = sums.reshape(NZ, RIM, 128)
+        slot_send[...] = slot_sum[...].astype(BF16)
+        for d in range(1, NZ):
+            send(
+                slot_send.at[lax.rem(z + d, NZ)],
+                slot_in.at[d - 1],
+                small_s.at[3],
+                small_r.at[3],
+                to["z"](d),
+            )
+        await_bytes(bias_in, small_r.at[1])
+        total = bias[...]
+        for d in range(NZ - 1):
+            total += bias_in[d]
+        bias_out[y] = total
+        send(bias_out.at[y], bias_out.at[y], small_s.at[4], small_r.at[4], to["y"](1))
+
+    def put(j):
+        some = pl.ds(JOBS[j][0], JOBS[j][1] - JOBS[j][0])
+        return pltpu.make_async_copy(grad_all.at[some], grad_hbm.at[some], out_sems.at[j])
+
+    def ring(step):
+        for j in range(len(JOBS)):
+            if on_ring(j, 2):
+                for side in range(2):
+                    if step <= ring_steps(j)[side]:
+                        ring_wait(j, step, side)
+                    if step < ring_steps(j)[side]:
+                        ring_send(j, step + 1, side)
+                if step == NZ // 2:
+                    put(j).start()
+
+    moves = {"sum": sum_over_z, "go": advance, "ring": ring, "slots": slots}
+    for name, *at in SCHEDULE:
+        moves[name](*at)
+    for j in range(len(JOBS)):
+        if not on_ring(j, 2):
+            gathered(j, 2)
+            put(j).start()
     await_bytes(slot_in, small_r.at[3])
     total = slot_sum[z]
     for d in range(NZ - 1):
         total += slot_in[d].astype(F32)
     side_out[...] = total
     stores[4].start()
-    for step in range(1, NZ // 2 + 1):
-        for o in range(9):
-            if on_ring(o, 2):
-                for side in range(2):
-                    if step <= ring_steps(o)[side]:
-                        ring_wait(o, step, side)
-                    if step < ring_steps(o)[side]:
-                        ring_send(o, step + 1, side)
-                if step == NZ // 2:
-                    put(o).start()
-            elif step == 3:
-                gathered(o, 2)
-                put(o).start()
     await_bytes(bias, small_r.at[4])
     stores[5].start()
     for store in stores:
         store.wait()
-    for o in range(9):
-        put(o).wait()
+    for j in range(len(JOBS)):
+        put(j).wait()
 
     await_bytes(dpad_in, small_s.at[0])
     await_bytes(bias_in, small_s.at[1])
@@ -679,15 +710,15 @@
         await_bytes(near.at[pl.ds(0, NQ - 1)], small_s.at[sem])
     for g, (low, high) in enumerate(GROUPS):
         await_bytes(grad_in.at[:, pl.ds(low, high - low)], sum_s.at[g])
-    for o in range(9):
+    for j in range(len(JOBS)):
         for stage in range(3):
-            if not on_ring(o, stage):
-                await_bytes(stage_bytes(o, stage), all_s.at[o, stage])
+            if not on_ring(j, stage):
+                await_bytes(stage_bytes(j, stage), all_s.at[j, stage])
                 continue
             for side in range(2):
-                for step in range(ring_steps(o)[side]):
+                for step in range(ring_steps(j)[side]):
                     await_bytes(
-                        bytes_of(box_rows("xy")), ring_s.at[o, side * (NZ // 2) + step]
+                        bytes_of(box_rows(j, "xy")), ring_s.at[j, side * (NZ // 2) + step]
                     )
 
 
@@ -732,7 +763,7 @@
         pltpu.VMEM((9, 128, 128), BF16),
         pltpu.VMEM((NZ - 1, 9, SHARE, 128), BF16),
         pltpu.VMEM((9, NX, NY, NZ, SHARE, 128), BF16),
-        pltpu.VMEM((1024, 128), BF16),
+        pltpu.VMEM((9 * 1024, 128), BF16),
         pltpu.VMEM((8, 128), F32),
         pltpu.VMEM((NC, DROWS, 128), BF16),
         pltpu.VMEM((NC - 1, DROWS, 128), BF16),
@@ -746,9 +777,9 @@
         pltpu.VMEM((NZ * RIM, NQ * 128), BF16),
         pltpu.VMEM((NZ - 1, 8, 128), F32),
     ]
-    for shape in ((12,), (len(GROUPS),), (9, 3), (9, NZ)):
+    for shape in ((12,), (len(GROUPS),), (len(JOBS), 3), (len(JOBS), NZ)):
         scratch += [pltpu.SemaphoreType.DMA(shape)] * 2
-    for count in (9, len(operands), len(results) - 1):
+    for count in (len(JOBS), len(operands), len(results) - 1):
         scratch.append(pltpu.SemaphoreType.DMA((count,)))
     return pl.pallas_call(
         whole_kernel,

time: 78 us -> 77.8 us (level)
  no operation moved by 1% of the time
where the time goes in v5:
time: 77.8 us; the launch traced here: 76.5 us
  Pallas kernels  75.9 us (98%)
    pallas_call x1, Pallas kernels, whole(): pl.pallas_call(whole_kernel, out_shape=results, in_specs=[hbm] * len(oper...  72.4 us
    pallas_call x1, Pallas kernels, finish(): pl.pallas_call(finish_kernel, out_shape=(jax.ShapeDtypeStruct(state, BF16...  3.54 us

profile of v5, /device:TPU:32, one launch (start us, length us, event | category | flops | bytes accessed | tf_op | source)
XLA Modules:
  0.0 76.5 jit_solution(6049663836169009206)
XLA Ops:
  0.6 72.4 %whole.1 = (bf16[3,64,64]{2,1,0:T(8,128)(2,1)}, f32[3,64,64]{2,1,0:T(8,128)}, f32[3,64,64]{2,1,0:T(8,128)}, bf16[9,4,2,8,16,128]{5,4,3,2,1,0:T(8,128)(2,1)}, f32...) custom-call(bf16[3,64,64]{2,1,0:T(8,128)(2,1)} %inp_hbm.1, bf16[3,64,64]{2,1,0:T(8,128)(2,1)} %hid_hbm.1, ...), custom_call_target="tpu_custom_call" | custom-call | tf_op jit(solution)/shard_map/whole/pallas_call | solution.py:784
  73.0 3.5 %finish.1 = (bf16[3,64,64]{2,1,0:T(8,128)(2,1)}, f32[3,64,64]{2,1,0:T(8,128)}, f32[3,64,64]{2,1,0:T(8,128)}, f32[9,256,512]{2,1,0:T(8,128)}, f32[4,64]{1,0:T(4,1...) custom-call(bf16[3,64,64]{2,1,0:T(8,128)(2,1)} %get-tuple-element.21.hidden_hbm, ...), custom_call_target="tpu_custom_call" | custom-call | tf_op jit(solution)/shard_map/finish/pallas_call | solution.py:891

commit v6 on v4

--- a/solution.py
+++ b/solution.py
@@ -20,7 +20,7 @@
 DROWS = BODY + 64
 SHARE = 16
 GROUPS = ((0, 3), (3, 6), (6, 9))
-ORDERS = ("yxz", "zyx", "yxz", "zxy", "yxz", "zyx", "yxz", "zxy", "zyx")
+ORDERS = ("yxz", "yxz", "yxz", "zxy", "zxy", "zxy", "zyx", "zyx", "zyx")
 VMEM_LIMIT = 56 * 1024 * 1024
 
 
@@ -640,12 +640,6 @@
         for o in range(9):
             gathered(o, stage)
             gather(o, stage + 1)
-    await_bytes(slot_in, small_r.at[3])
-    total = slot_sum[z]
-    for d in range(NZ - 1):
-        total += slot_in[d].astype(F32)
-    side_out[...] = total
-    stores[4].start()
     for step in range(1, NZ // 2 + 1):
         for o in range(9):
             if on_ring(o, 2):
@@ -659,6 +653,12 @@
             elif step == 3:
                 gathered(o, 2)
                 put(o).start()
+    await_bytes(slot_in, small_r.at[3])
+    total = slot_sum[z]
+    for d in range(NZ - 1):
+        total += slot_in[d].astype(F32)
+    side_out[...] = total
+    stores[4].start()
     await_bytes(bias, small_r.at[4])
     stores[5].start()
     for store in stores:

time: 78 us -> 77.4 us (level)
  Pallas kernels: 76.6 us -> 75.8 us
    pallas_call x1, Pallas kernels: 73.1 us -> 72.2 us  [whole(): pl.pallas_call(whole_kernel, out_shape=results, in_specs=[hbm] * len(oper...]
where the time goes in v6:
time: 77.4 us; the launch traced here: 76.4 us
  Pallas kernels  75.8 us (98%)
    pallas_call x1, Pallas kernels, whole(): pl.pallas_call(whole_kernel, out_shape=results, in_specs=[hbm] * len(oper...  72.2 us
    pallas_call x1, Pallas kernels, finish(): pl.pallas_call(finish_kernel, out_shape=(jax.ShapeDtypeStruct(state, BF16...  3.54 us

profile of v6, /device:TPU:32, one launch (start us, length us, event | category | flops | bytes accessed | tf_op | source)
XLA Modules:
  0.0 76.4 jit_solution(8485380255249577382)
XLA Ops:
  0.6 72.2 %whole.1 = (bf16[3,64,64]{2,1,0:T(8,128)(2,1)}, f32[3,64,64]{2,1,0:T(8,128)}, f32[3,64,64]{2,1,0:T(8,128)}, bf16[9,4,2,8,16,128]{5,4,3,2,1,0:T(8,128)(2,1)}, f32...) custom-call(bf16[3,64,64]{2,1,0:T(8,128)(2,1)} %inp_hbm.1, bf16[3,64,64]{2,1,0:T(8,128)(2,1)} %hid_hbm.1, ...), custom_call_target="tpu_custom_call" | custom-call | tf_op jit(solution)/shard_map/whole/pallas_call | solution.py:753
  72.9 3.5 %finish.1 = (bf16[3,64,64]{2,1,0:T(8,128)(2,1)}, f32[3,64,64]{2,1,0:T(8,128)}, f32[3,64,64]{2,1,0:T(8,128)}, f32[9,256,512]{2,1,0:T(8,128)}, f32[4,64]{1,0:T(4,1...) custom-call(bf16[3,64,64]{2,1,0:T(8,128)(2,1)} %get-tuple-element.21.hidden_hbm, ...), custom_call_target="tpu_custom_call" | custom-call | tf_op jit(solution)/shard_map/finish/pallas_call | solution.py:860
